TPU v7x, 256 devices: a whole 4x4x8 slice. The times are simulated.
256 devices in a mesh: row: 16 (over z, core), col: 16 (over y, x).
Axes of the slice: x: 4, y: 4, z: 8, core: 2. Of those that a mesh axis runs over, the one named last changes fastest.
Arguments:
- matrix: float32 [196608, 2048], P('row', 'col')
- plan: int32 [16], replicated, may hold values from 0 to 1
Outputs:
- rotated_matrix: float32 [196608, 2048], P('row', 'col')
Inputs may be any that keep to these rules, and one draw needn't show every extreme that they name: `plan`: entry p picks block 2p (0) or block 2p+1 (1) of pair p.
All inputs are finite; a program needn't handle non-finite values.
Results may differ from a plain program's by a relative error of at most 0.0003.
Values sent between devices are 32-bit elements; how exact they have to be, the bound alone decides.
No kernel may reach another device: no remote copies, remote signals or barrier semaphores. Data moves between devices by JAX's collectives and lax.ppermute only.
A program may use at most 128 MiB of HBM per device.

v0:
```python
import jax
import jax.numpy as jnp
from jax import lax
from jax.sharding import PartitionSpec as P

ITERS = 3


def passed_along(array, axis, by):
    size = lax.axis_size(axis)
    return lax.ppermute(array, axis, [(i, (i + by) % size) for i in range(size)])


def rotation(gram_matrix):
    order = gram_matrix.shape[0]
    basis = jnp.eye(order, dtype=jnp.float32)
    for step_index in range(ITERS):
        product = jnp.dot(
            gram_matrix, basis, precision=lax.Precision.HIGHEST, preferred_element_type=jnp.float32
        )
        normal_eq = jnp.dot(
            product.T, product, precision=lax.Precision.HIGHEST, preferred_element_type=jnp.float32
        )
        factor = jnp.linalg.cholesky(normal_eq)
        basis = lax.linalg.triangular_solve(
            factor, product, left_side=False, lower=True, transpose_a=True
        )
    return basis


def local_gram(columns):
    return jnp.dot(
        columns.T, columns, precision=lax.Precision.HIGHEST, preferred_element_type=jnp.float32
    )


def apply_turn(columns, turn_cols):
    return jnp.dot(
        columns, turn_cols, precision=lax.Precision.HIGHEST, preferred_element_type=jnp.float32
    )


def local(matrix, plan):
    width_cols = matrix.shape[1] // 2
    gram_total = lax.psum(local_gram(matrix), "row")
    turned = apply_turn(matrix, rotation(gram_total))
    leaver = plan[lax.axis_index("col")] == 1
    front_half = turned[:, :width_cols]
    back_half = turned[:, width_cols:]
    leaving = jnp.where(leaver, back_half, front_half)
    staying = jnp.where(leaver, front_half, back_half)
    arrived = passed_along(leaving, "col", 1)
    joined = jnp.concatenate([staying, arrived], axis=1)
    pair_total = lax.psum(local_gram(joined), "row")
    rotated = apply_turn(joined, rotation(pair_total))
    new_stay = rotated[:, :width_cols]
    new_leave = passed_along(rotated[:, width_cols:], "col", -1)
    return jnp.where(
        leaver,
        jnp.concatenate([new_stay, new_leave], axis=1),
        jnp.concatenate([new_leave, new_stay], axis=1),
    )


def solution(mesh):
    in_specs = (P("row", "col"), P())
    out_specs = P("row", "col")
    return jax.shard_map(local, mesh=mesh, in_specs=in_specs, out_specs=out_specs, check_vma=False)
```

profile of v0, /device:TPU:1, one launch (start us, length us, event | category | flops | bytes accessed | tf_op | source)
XLA Modules:
  0.0 554.4 jit_solution(6457672009077889745)
XLA Ops:
  6.5 15.5 %fusion.29 = f32[128,128]{1,0:T(8,128)} fusion(f32[12288,128]{1,0:T(8,128)} %param.5), kind=kOutput, calls=%fused_computation.64 | convolution fusion | flops 2415919104 | bytes 6356992 | tf_op jit(solution)/shard_map/dot_general | solution.py:32
  22.1 0.3 all-reduce.5.cloned.1.call-start
  22.4 0.6 dynamic_slice.3
  23.6 101.7 %all-reduce.3.cloned.1.call-done = f32[128,128]{1,0:T(8,128)} async-done(((f32[128,128]{1,0:T(8,128)}), f32[128,128]{1,0:T(8,128)}) %all-reduce.3.cloned.1.call-update) | async-done | bytes 65552 | tf_op jit(solution)/shard_map/psum | solution.py:45
  125.3 1.0 fusion.21
  126.4 0.3 fusion.30
  126.7 0.1 copy.3
  126.8 11.7 %cholesky.104 = f32[128,128]{1,0:T(8,128)S(1)} custom-call(f32[128,128]{1,0:T(8,128)S(1)} %fusion.19), custom_call_target="Cholesky" | custom-call | tf_op jit(solution)/shard_map/jit(cholesky)/cholesky | solution.py:24
  138.5 0.6 compare_reduce_fusion.5
  139.2 0.7 fusion.2
  139.8 9.8 %custom-call.10 = f32[1,128,128]{1,2,0:T(8,128)S(1)} custom-call(f32[1,128,128]{2,1,0:T(8,128)S(1)} %fusion.2), custom_call_target="InvertDiagBlocksLowerTriangular" | custom-call | tf_op jit(solution)/shard_map/triangular_solve/custom-call.0 | solution.py:25
  149.6 0.3 convolution_bitcast_fusion.6
  149.9 1.1 fusion.31
  151.0 0.3 fusion.32
  151.5 11.7 %cholesky.115 = f32[128,128]{1,0:T(8,128)S(1)} custom-call(f32[128,128]{1,0:T(8,128)S(1)} %fusion.17), custom_call_target="Cholesky" | custom-call | tf_op jit(solution)/shard_map/jit(cholesky)/cholesky | solution.py:24
  163.2 0.6 compare_reduce_fusion.4
  163.8 0.7 fusion.3
  164.5 10.2 %custom-call.11 = f32[1,128,128]{1,2,0:T(8,128)S(1)} custom-call(f32[1,128,128]{2,1,0:T(8,128)S(1)} %fusion.3), custom_call_target="InvertDiagBlocksLowerTriangular" | custom-call | tf_op jit(solution)/shard_map/triangular_solve/custom-call.0 | solution.py:25
  174.7 0.3 convolution_bitcast_fusion.5
  175.0 1.1 fusion.33
  176.1 0.3 fusion.34
  176.4 0.1 copy.5
  176.5 11.7 %cholesky.126 = f32[128,128]{1,0:T(8,128)S(1)} custom-call(f32[128,128]{1,0:T(8,128)S(1)} %fusion.15), custom_call_target="Cholesky" | custom-call | tf_op jit(solution)/shard_map/jit(cholesky)/cholesky | solution.py:24
  188.3 0.6 compare_reduce_fusion.3
  188.9 0.7 fusion.4
  189.6 9.8 %custom-call.12 = f32[1,128,128]{1,2,0:T(8,128)S(1)} custom-call(f32[1,128,128]{2,1,0:T(8,128)S(1)} %fusion.4), custom_call_target="InvertDiagBlocksLowerTriangular" | custom-call | tf_op jit(solution)/shard_map/triangular_solve/custom-call.0 | solution.py:25
  199.4 0.3 convolution_bitcast_fusion.4
  199.7 7.8 %convolution_bitcast_fusion = f32[12288,128]{0,1:T(8,128)S(1)} fusion(f32[128,128]{0,1:T(8,128)S(1)} %convolution_bitcast_fusion.4, f32[12288,128]{1,0:T(8,128)} %param.5), kind=kOutput, calls=%fused_computation | convolution fusion | flops 2415919104 | bytes 12648448 | tf_op jit(solution)/shard_map/dot_general | solution.py:38
  207.5 0.4 slice_select_fusion.1
  207.9 1.4 collective-permute-start
  209.4 71.7 %collective-permute-done = f32[12288,64]{0,1:T(8,128)S(1)} collective-permute-done((f32[12288,64]{0,1:T(8,128)S(1)}, f32[12288,64]{0,1:T(8,128)S(1)}, u32[]{:S(2)}, u32[]{:S(2)}) %collective-permute-start) | collective-permute-done | bytes 3145760 | tf_op jit(solution)/shard_map/ppermute | solution.py:11
  281.1 1.7 copy-done
  282.7 5.6 %fusion.1 = f32[128,128]{1,0:T(8,128)} fusion(f32[12288,64]{0,1:T(8,128)S(1)} %collective-permute-done, f32[12288,64]{0,1:T(8,128)S(1)} %get-tuple-element.9), kind=kOutput, calls=%fused_computation.4 | convolution fusion | flops 2417491968 | bytes 6356992 | tf_op jit(solution)/shard_map/dot_general | solution.py:32
  288.4 93.8 %all-reduce.5.cloned.1.call-done = f32[128,128]{1,0:T(8,128)} async-done(((f32[128,128]{1,0:T(8,128)}), f32[128,128]{1,0:T(8,128)}) %all-reduce.5.cloned.1.call-update) | async-done | bytes 65552 | tf_op jit(solution)/shard_map/psum | solution.py:54
  382.2 1.0 fusion.20
  383.2 0.3 fusion.35
  383.5 0.1 copy.6
  383.7 11.7 %cholesky.137 = f32[128,128]{1,0:T(8,128)S(1)} custom-call(f32[128,128]{1,0:T(8,128)S(1)} %fusion.13), custom_call_target="Cholesky" | custom-call | tf_op jit(solution)/shard_map/jit(cholesky)/cholesky | solution.py:24
  395.4 0.7 compare_reduce_fusion.2
  396.1 0.6 fusion.5
  396.7 9.8 %custom-call.13 = f32[1,128,128]{1,2,0:T(8,128)S(1)} custom-call(f32[1,128,128]{2,1,0:T(8,128)S(1)} %fusion.5), custom_call_target="InvertDiagBlocksLowerTriangular" | custom-call | tf_op jit(solution)/shard_map/triangular_solve/custom-call.0 | solution.py:25
  406.5 0.3 convolution_bitcast_fusion.3
  406.8 1.1 fusion.36
  407.9 0.5 fusion.37
  408.4 0.1 copy.7
  408.5 11.7 %cholesky.148 = f32[128,128]{1,0:T(8,128)S(1)} custom-call(f32[128,128]{1,0:T(8,128)S(1)} %fusion.11), custom_call_target="Cholesky" | custom-call | tf_op jit(solution)/shard_map/jit(cholesky)/cholesky | solution.py:24
  420.3 0.7 compare_reduce_fusion.1
  420.9 0.6 fusion.6
  421.6 9.8 %custom-call.14 = f32[1,128,128]{1,2,0:T(8,128)S(1)} custom-call(f32[1,128,128]{2,1,0:T(8,128)S(1)} %fusion.6), custom_call_target="InvertDiagBlocksLowerTriangular" | custom-call | tf_op jit(solution)/shard_map/triangular_solve/custom-call.0 | solution.py:25
  431.4 0.3 convolution_bitcast_fusion.2
  431.7 1.1 fusion.38
  432.8 0.3 fusion.39
  433.1 0.1 copy.8
  433.2 11.7 %cholesky.159 = f32[128,128]{1,0:T(8,128)S(1)} custom-call(f32[128,128]{1,0:T(8,128)S(1)} %fusion.9), custom_call_target="Cholesky" | custom-call | tf_op jit(solution)/shard_map/jit(cholesky)/cholesky | solution.py:24
  444.9 0.7 compare_reduce_fusion
  445.7 0.7 fusion.7
  446.4 10.0 %custom-call.15 = f32[1,128,128]{1,2,0:T(8,128)S(1)} custom-call(f32[1,128,128]{2,1,0:T(8,128)S(1)} %fusion.7), custom_call_target="InvertDiagBlocksLowerTriangular" | custom-call | tf_op jit(solution)/shard_map/triangular_solve/custom-call.0 | solution.py:25
  456.4 0.3 convolution_bitcast_fusion.1
  456.7 8.2 %fusion = f32[12288,128]{0,1:T(8,128)S(1)} fusion(f32[128,128]{0,1:T(8,128)S(1)} %convolution_bitcast_fusion.1, f32[12288,64]{0,1:T(8,128)} %copy-done, f32[12288,64]{0,1:T(8,128)S(1)} %get-tuple-element.9), kind=kOutput, calls=%fused_computation.3 | convolution fusion | flops 2417491968 | bytes 12648448 | tf_op jit(solution)/shard_map/dot_general | solution.py:38
  464.9 0.6 fusion.28
  465.5 4.7 collective-permute-start.1
  470.2 67.4 %collective-permute-done.1 = f32[12288,64]{0,1:T(8,128)S(1)} collective-permute-done((f32[12288,64]{0,1:T(8,128)S(1)}, f32[12288,64]{0,1:T(8,128)S(1)}, u32[]{:S(2)}, u32[]{:S(2)}) %collective-permute-start.1) | collective-permute-done | bytes 3145760 | tf_op jit(solution)/shard_map/ppermute | solution.py:11
  537.6 3.0 maximum_select_fusion
  540.6 6.6 %copy.9 = f32[12288,128]{1,0:T(8,128)} copy(f32[12288,128]{0,1:T(8,128)} %maximum_select_fusion) | data formatting | bytes 12582912 | tf_op jit(solution)/shard_map/jit(_where)/select_n | solution.py:58
  (19 shorter events, 0.4 us)
Async XLA Ops:
  6.5 15.8 %copy-start.1 = (s32[16]{0:T(128)S(1)}, s32[16]{0:T(128)}, u32[]{:S(2)}) copy-start(s32[16]{0:T(128)} %param.6) | copy-start | bytes 196
  6.5 118.8 %all-reduce.3.cloned.1.call-start = ((), (), s32[]{:S(2)}) async-start(), calls=%async_computation | async-start | bytes 131072 | tf_op jit(solution)/shard_map/psum | solution.py:45
  22.1 360.1 %all-reduce.5.cloned.1.call-start = ((), (), s32[]{:S(2)}) async-start(), calls=%async_computation.1 | async-start | bytes 131072 | tf_op jit(solution)/shard_map/psum | solution.py:54
  207.9 73.1 %collective-permute-start = (f32[12288,64]{0,1:T(8,128)S(1)}, f32[12288,64]{0,1:T(8,128)S(1)}, u32[]{:S(2)}, u32[]{:S(2)}) collective-permute-start(f32[12288,64]{0,1:T(8,128)S(1)} %get-tuple-element.10), channel_id=1, source_target_pairs={{0,1},{1,2},{2,3},{3,4},{4,5},{5,6},{6,7},{7,8},{8,9},{9,10},{10,1... | collective-permute-start | bytes 9437192 | tf_op jit(solution)/shard_map/ppermute | solution.py:11
  281.1 1.7 copy-start
  465.5 72.0 %collective-permute-start.1 = (f32[12288,64]{0,1:T(8,128)S(1)}, f32[12288,64]{0,1:T(8,128)S(1)}, u32[]{:S(2)}, u32[]{:S(2)}) collective-permute-start(f32[12288,64]{0,1:T(8,128)S(1)} %get-tuple-element.8), channel_id=1, source_target_pairs={{0,15},{1,0},{2,1},{3,2},{4,3},{5,4},{6,5},{7,6},{8,7},{9,8},{10,9... | collective-permute-start | bytes 9437192 | tf_op jit(solution)/shard_map/ppermute | solution.py:11
Sparse Core Ops, SparseCore 0:
  22.2 103.0 all-reduce.2
  288.5 93.6 all-reduce.4
where the time goes:
time: 559 us; the launch traced here: 554 us
  waiting for transfers between devices  335 us (60%)
  other arithmetic  141 us (25%)
  matrix products  47.4 us (8%)
  between operations  14.8 us (3%)
  local copies, waits for them, and re-layouts  9.94 us (2%)
  starting transfers between devices  6.36 us (1%)
    ppermute x2, waiting for transfers between devices, passed_along(): lax.ppermute(array, axis, [(i, (i + by) % size) for i in range(size)])  139 us
    psum x1, waiting for transfers between devices, local(): gram_total = lax.psum(local_gram(matrix), 'row')  102 us
    psum x1, waiting for transfers between devices, local(): pair_total = lax.psum(local_gram(joined), 'row')  93.8 us
    another operation x18, other arithmetic, rotation(): factor = jnp.linalg.cholesky(normal_eq)  74.5 us
    another operation x12, other arithmetic, rotation(): lax.linalg.triangular_solve(factor, product, left_side=False, lower=True,...  63.4 us
    dot_general x2, matrix products, local_gram(): jnp.dot(columns.T, columns, precision=lax.Precision.HIGHEST, preferred_el...  21.2 us
    dot_general x2, matrix products, apply_turn(): jnp.dot(columns, turn_cols, precision=lax.Precision.HIGHEST, preferred_el...  16.1 us
  transfers between devices with their start and end apart: 4, of which 4 were waited for; matrix products, arithmetic and copies ran while one was open for 0% of the time, Pallas kernels for 0%

commit v1 on v0

v1 whole, which is shorter than its diff:
```python
import functools

import jax
import jax.numpy as jnp
from jax import lax
from jax.experimental import pallas as pl
from jax.experimental.pallas import tpu as pltpu
from jax.sharding import PartitionSpec as P

ITERS = 3
ORDER = 128
HALF = 64
GROUP = 8
GRAM_ROWS = 1024
TURN_ROWS = 1024
F32 = jnp.float32
BF16 = jnp.bfloat16


def split_two(value):
    high = value.astype(BF16)
    low = (value - high.astype(F32)).astype(BF16)
    return high, low


def split_three(value):
    high = value.astype(BF16)
    rest = value - high.astype(F32)
    middle = rest.astype(BF16)
    low = (rest - middle.astype(F32)).astype(BF16)
    return high, middle, low


def dot_bf16(left, right, dims):
    return lax.dot_general(left, right, (dims, ((), ())), preferred_element_type=F32)


def dot_six(left, right, transpose_right):
    lh, lm, ll = split_three(left)
    rh, rm, rl = split_three(right)
    axis = 1 if transpose_right else 0
    dims = ((1,), (axis,))
    total = None
    for (la, ra), (lb, rb) in (((lh, rl), (ll, rh)), ((lm, rm), (lm, rh)), ((lh, rm), (lh, rh))):
        term = dot_bf16(
            jnp.concatenate([la, lb], axis=1), jnp.concatenate([ra, rb], axis=axis), dims
        )
        total = term if total is None else total + term
    return total


def across(column, rows):
    return jnp.broadcast_to(column, (rows, ORDER))


def orthonormal_rows(normal, rows_in):
    done = []
    spot = lax.broadcasted_iota(jnp.int32, (GROUP, ORDER), 0)
    for start in range(0, ORDER, GROUP):
        tail = ORDER - start - GROUP
        head_n, head_y = normal[:GROUP], rows_in[:GROUP]
        tail_n, tail_y = normal[GROUP:], rows_in[GROUP:]
        head_c = [across(head_n[:, start + j : start + j + 1], GROUP) for j in range(GROUP)]
        tail_c = [across(tail_n[:, start + j : start + j + 1], tail) for j in range(GROUP)] if tail else []
        pivots = head_c[0]
        for k in range(GROUP):
            pivot = across(head_c[k][k : k + 1], GROUP)
            inverse = 1.0 / pivot
            row_n = head_n[k : k + 1]
            row_y = head_y[k : k + 1]
            if k:
                pivots = jnp.where(spot >= k, pivot, pivots)
            else:
                pivots = pivot
            cross = [head_c[j][k : k + 1] for j in range(k + 1, GROUP)]
            if k < GROUP - 1:
                scaled = jnp.where(spot > k, head_c[k] * inverse, 0.0)
                head_n = head_n - scaled * row_n
                head_y = head_y - scaled * row_y
                for j in range(k + 1, GROUP):
                    head_c[j] = head_c[j] - scaled * cross[j - k - 1]
            if tail:
                scaled = tail_c[k] * inverse[:1]
                tail_n = tail_n - scaled * row_n
                tail_y = tail_y - scaled * row_y
                for j in range(k + 1, GROUP):
                    tail_c[j] = tail_c[j] - scaled * cross[j - k - 1]
        done.append(head_y * lax.rsqrt(pivots))
        normal, rows_in = tail_n, tail_y
    return jnp.concatenate(done, axis=0)


def rotation_kernel(gram_ref, out_ref):
    gram = gram_ref[...]
    gram = gram * (1.0 / jnp.max(jnp.abs(gram)))

    def turn(rows):
        out_ref[...] = orthonormal_rows(dot_six(rows, rows, True), rows)

    turn(gram)

    def step(_, carry):
        turn(dot_six(out_ref[...], gram, False))
        return carry

    lax.fori_loop(1, ITERS, step, 0)


def rotation_rows(gram_total):
    return pl.pallas_call(
        rotation_kernel,
        out_shape=jax.ShapeDtypeStruct((ORDER, ORDER), F32),
        in_specs=[pl.BlockSpec(memory_space=pltpu.VMEM)],
        out_specs=pl.BlockSpec(memory_space=pltpu.VMEM),
        compiler_params=pltpu.CompilerParams(vmem_limit_bytes=32 * 2**20),
        name="rotation",
    )(gram_total)


def gram_kernel(x_ref, out_ref, total):
    step = pl.program_id(0)

    @pl.when(step == 0)
    def _():
        total[...] = jnp.zeros_like(total)

    high, low = split_two(x_ref[...])
    both = jnp.concatenate([high, low], axis=1)
    total[...] += dot_bf16(high, both, ((0,), (0,)))

    @pl.when(step == pl.num_programs(0) - 1)
    def _():
        mixed = total[:, ORDER:]
        out_ref[...] = total[:, :ORDER] + (mixed + mixed.T)


def gram_of(columns):
    rows = columns.shape[0]
    return pl.pallas_call(
        gram_kernel,
        grid=(rows // GRAM_ROWS,),
        out_shape=jax.ShapeDtypeStruct((ORDER, ORDER), F32),
        in_specs=[pl.BlockSpec((GRAM_ROWS, ORDER), lambda i: (i, 0))],
        out_specs=pl.BlockSpec((ORDER, ORDER), lambda i: (0, 0)),
        scratch_shapes=[pltpu.VMEM((ORDER, 2 * ORDER), F32)],
        compiler_params=pltpu.CompilerParams(vmem_limit_bytes=32 * 2**20),
        name="gram",
    )(columns)


def turn_kernel(flag_ref, rows_ref, top_ref, bottom_ref, early_ref, late_ref, high, low):
    @pl.when(pl.program_id(0) == 0)
    def _():
        front, back = rows_ref[:HALF], rows_ref[HALF:]
        is_back = flag_ref[0] == 1
        early = jnp.where(is_back, back, front)
        late = jnp.where(is_back, front, back)
        none = jnp.zeros_like(early)
        weights = jnp.concatenate(
            [
                jnp.concatenate([early, none, late, none], axis=0),
                jnp.concatenate([none, early, none, late], axis=0),
            ],
            axis=1,
        ).T
        high[...], low[...] = split_two(weights)

    xh, xl = split_two(jnp.concatenate([top_ref[...], bottom_ref[...]], axis=1))
    dims = ((1,), (0,))
    out = dot_bf16(xh, high[...], dims) + (dot_bf16(xh, low[...], dims) + dot_bf16(xl, high[...], dims))
    early_ref[...] = out[:, :ORDER]
    late_ref[...] = out[:, ORDER:]


def turn(columns, turn_rows, early_is_back):
    rows = columns.shape[0] // 2
    steps = rows // TURN_ROWS
    packed = jax.ShapeDtypeStruct((rows, ORDER), F32)
    block = (TURN_ROWS, ORDER)
    return pl.pallas_call(
        turn_kernel,
        grid=(steps,),
        out_shape=(packed, packed),
        in_specs=[
            pl.BlockSpec(memory_space=pltpu.SMEM),
            pl.BlockSpec((ORDER, ORDER), lambda i: (0, 0)),
            pl.BlockSpec(block, lambda i: (i, 0)),
            pl.BlockSpec(block, lambda i: (i + steps, 0)),
        ],
        out_specs=(pl.BlockSpec(block, lambda i: (i, 0)), pl.BlockSpec(block, lambda i: (i, 0))),
        scratch_shapes=[pltpu.VMEM((2 * ORDER, 2 * ORDER), BF16)] * 2,
        compiler_params=pltpu.CompilerParams(vmem_limit_bytes=32 * 2**20),
        name="turn",
    )(early_is_back, turn_rows, columns, columns)


def half_roll(value, axis):
    return pltpu.roll(value, HALF, axis)


def low_lanes(shape):
    return lax.broadcasted_iota(jnp.int32, shape, 1) < HALF


def pair_gram_kernel(core_ref, own_ref, come_ref, out_ref, total):
    step = pl.program_id(0)

    @pl.when(step == 0)
    def _():
        total[...] = jnp.zeros_like(total)

    high, low = split_two(jnp.concatenate([own_ref[...], come_ref[...]], axis=1))
    total[...] += dot_bf16(high, jnp.concatenate([high, low], axis=1), ((0,), (0,)))

    @pl.when(step == pl.num_programs(0) - 1)
    def _():
        mixed = total[:, 2 * ORDER :]
        whole = total[:, : 2 * ORDER] + (mixed + mixed.T)
        tops = jnp.concatenate([whole[:HALF], whole[ORDER : ORDER + HALF]], axis=0)
        bottoms = jnp.concatenate([whole[HALF:ORDER], whole[ORDER + HALF :]], axis=0)
        first = low_lanes((ORDER, ORDER))
        gram = jnp.where(first, tops[:, :ORDER], half_roll(tops[:, ORDER:], 1)) + jnp.where(
            first, half_roll(bottoms[:, :ORDER], 1), bottoms[:, ORDER:]
        )
        swapped = half_roll(half_roll(gram, 1), 0)
        out_ref[...] = jnp.where(core_ref[0] == 1, swapped, gram)


def pair_gram(core, own, come):
    rows = own.shape[0]
    block = pl.BlockSpec((GRAM_ROWS, ORDER), lambda i: (i, 0))
    return pl.pallas_call(
        pair_gram_kernel,
        grid=(rows // GRAM_ROWS,),
        out_shape=jax.ShapeDtypeStruct((ORDER, ORDER), F32),
        in_specs=[pl.BlockSpec(memory_space=pltpu.SMEM), block, block],
        out_specs=pl.BlockSpec((ORDER, ORDER), lambda i: (0, 0)),
        scratch_shapes=[pltpu.VMEM((2 * ORDER, 4 * ORDER), F32)],
        compiler_params=pltpu.CompilerParams(vmem_limit_bytes=32 * 2**20),
        name="pair_gram",
    )(core, own, come)


def finish_kernel(
    flags_ref, mine_ref, other_ref, early_ref, late_ref, come_ref, last_ref, out_ref, high, low
):
    @pl.when(pl.program_id(0) == 0)
    def _():
        swap = flags_ref[1] == 1

        def ordered(rows):
            return jnp.where(swap, half_roll(half_roll(rows, 1), 0), rows)

        first = low_lanes((HALF, ORDER))
        none = jnp.zeros((HALF, ORDER), F32)
        late_rows = ordered(mine_ref[...])[:HALF]
        early_rows = ordered(other_ref[...])[HALF:]
        late_own, late_come = jnp.where(first, late_rows, 0.0), jnp.where(first, 0.0, late_rows)
        early_last, early_own = jnp.where(first, early_rows, 0.0), jnp.where(first, 0.0, early_rows)

        def lanes(parts):
            return jnp.concatenate(parts, axis=1)

        early_top = lanes([half_roll(early_own, 1), none, none, early_last])
        early_bottom = lanes([early_own, none, none, half_roll(early_last, 1)])
        late_top = lanes([none, late_own, half_roll(late_come, 1), none])
        late_bottom = lanes([none, half_roll(late_own, 1), late_come, none])
        is_back = flags_ref[0] == 1
        weights = jnp.concatenate(
            [
                jnp.where(is_back, late_top, early_top),
                jnp.where(is_back, early_top, late_top),
                jnp.where(is_back, late_bottom, early_bottom),
                jnp.where(is_back, early_bottom, late_bottom),
            ],
            axis=0,
        ).T
        high[...], low[...] = split_two(weights)

    joined = jnp.concatenate([early_ref[...], late_ref[...], come_ref[...], last_ref[...]], axis=1)
    xh, xl = split_two(joined)
    dims = ((1,), (0,))
    out = dot_bf16(xh, high[...], dims) + (dot_bf16(xh, low[...], dims) + dot_bf16(xl, high[...], dims))
    out_ref[0] = out[:, :ORDER]
    out_ref[1] = out[:, ORDER:]


def finish(flags, mine, other, early, late, come, last):
    rows = early.shape[0]
    square = pl.BlockSpec((ORDER, ORDER), lambda i: (0, 0))
    block = pl.BlockSpec((TURN_ROWS, ORDER), lambda i: (i, 0))
    out = pl.pallas_call(
        finish_kernel,
        grid=(rows // TURN_ROWS,),
        out_shape=jax.ShapeDtypeStruct((2, rows, ORDER), F32),
        in_specs=[pl.BlockSpec(memory_space=pltpu.SMEM), square, square, block, block, block, block],
        out_specs=pl.BlockSpec((2, TURN_ROWS, ORDER), lambda i: (0, i, 0)),
        scratch_shapes=[pltpu.VMEM((4 * ORDER, 2 * ORDER), BF16)] * 2,
        compiler_params=pltpu.CompilerParams(vmem_limit_bytes=32 * 2**20),
        name="finish",
    )(flags, mine, other, early, late, come, last)
    return out.reshape(2 * rows, ORDER)


def moved(array, target):
    rows, cols = lax.axis_size("row"), lax.axis_size("col")
    pairs = []
    for row in range(rows):
        for col in range(cols):
            to_row, to_col = target(row, col)
            pairs.append((row * cols + col, (to_row % rows) * cols + to_col % cols))
    return lax.ppermute(array, ("row", "col"), pairs)


def outward(row, col):
    return row, col + (1 if row % 2 == 0 else -1)


def inward(row, col):
    return row, col + (-1 if row % 2 == 0 else 1)


def swap_rows(by):
    return lambda row, col: (row ^ by, col)


def partner(row, col):
    return (row + 1, col - 1) if row % 2 == 0 else (row - 1, col + 1)


def local(matrix, plan):
    core = lax.axis_index("row") % 2
    leaver = plan[lax.axis_index("col")]
    early_is_back = leaver ^ core
    gram = gram_of(matrix)
    for by in (1, 2, 4, 8):
        gram = gram + moved(gram, swap_rows(by))
    early, late = turn(matrix, rotation_rows(gram), early_is_back.reshape(1))
    come = moved(early, outward)
    late, come = lax.optimization_barrier((late, come))
    last = moved(late, inward)
    second = pair_gram(core.reshape(1), late, come)
    second = second + moved(second, partner)
    for by in (2, 4, 8):
        second = second + moved(second, swap_rows(by))
    mine = rotation_rows(second)
    other = moved(mine, swap_rows(1))
    return finish(jnp.stack([early_is_back, core]), mine, other, early, late, come, last)


def solution(mesh):
    in_specs = (P("row", "col"), P())
    out_specs = P("row", "col")
    return jax.shard_map(local, mesh=mesh, in_specs=in_specs, out_specs=out_specs, check_vma=False)
```

time: 559 us -> 169 us (0.30)
  waiting for transfers between devices: 335 us -> 86.4 us
  other arithmetic: 141 us -> 0.15 us
  matrix products: 47.4 us -> 0 us
  Pallas kernels: 0 us -> 44.2 us
  starting transfers between devices: 6.36 us -> 31 us
  between operations: 14.8 us -> 0.74 us
    psum x2 -> x0, waiting for transfers between devices: 196 us -> none  [the longest x1 102 us: local(): gram_total = lax.psum(local_gram(matrix), 'row')]
    another operation x30 -> x1, other arithmetic: 138 us -> 0.07 us  [local(): jnp.stack([early_is_back, core])]
    ppermute x2 -> x11, waiting for transfers between devices: 139 us -> 86.4 us  [moved(): return lax.ppermute(array, ('row', 'col'), pairs)]
    dot_general x16 -> x0, matrix products: 45.6 us -> none  [the longest x2 21.2 us: local_gram(): jnp.dot(columns.T, columns, precision=lax.Precision.HIGHEST, preferred_el...]
    pallas_call x0 -> x6, Pallas kernels: none -> 44.2 us  [the longest x2 25.8 us: rotation_rows(): pl.pallas_call(rotation_kernel, out_shape=jax.ShapeDtypeStruct((ORDER, OR...]
    ppermute x2 -> x11, starting transfers between devices: 6.11 us -> 31 us  [moved(): return lax.ppermute(array, ('row', 'col'), pairs)]
    select_n x1 -> x0, local copies, waits for them, and re-layouts: 6.55 us -> none  [local(): jnp.where(leaver, jnp.concatenate([new_stay, new_leave], axis=1), jnp.con...]
  transfers between devices with their start and end apart: 4 -> 11, of which waited for: 4 -> 10; matrix products, arithmetic and copies ran while one was open for 0% -> 0% of each run, Pallas kernels for 0% -> 10%
where the time goes in v1:
time: 169 us
  waiting for transfers between devices  86.4 us (51%)
  Pallas kernels  44.2 us (26%)
  starting transfers between devices  31 us (18%)
  local copies, waits for them, and re-layouts  6.19 us (4%)
    ppermute x11, waiting for transfers between devices, moved(): return lax.ppermute(array, ('row', 'col'), pairs)  86.4 us
    ppermute x11, starting transfers between devices, moved(): return lax.ppermute(array, ('row', 'col'), pairs)  31 us
    pallas_call x2, Pallas kernels, rotation_rows(): pl.pallas_call(rotation_kernel, out_shape=jax.ShapeDtypeStruct((ORDER, OR...  25.8 us
    pallas_call x1, Pallas kernels, finish(): pl.pallas_call(finish_kernel, grid=(rows // TURN_ROWS,), out_shape=jax.Sh...  8.01 us
    unnamed x6, local copies, waits for them, and re-layouts  5.58 us
    pallas_call x1, Pallas kernels, turn(): pl.pallas_call(turn_kernel, grid=(steps,), out_shape=(packed, packed), in...  3.71 us
    pallas_call x1, Pallas kernels, gram_of(): pl.pallas_call(gram_kernel, grid=(rows // GRAM_ROWS,), out_shape=jax.Shap...  3.52 us
  transfers between devices with their start and end apart: 11, of which 10 were waited for; matrix products, arithmetic and copies ran while one was open for 0% of the time, Pallas kernels for 10%

profile of v1, /device:TPU:1, one launch (start us, length us, event | category | flops | bytes accessed | tf_op | source)
XLA Modules:
  0.0 168.7 jit_solution(15471955553354644877)
XLA Ops:
  0.0 0.0 copy-start
  0.0 2.8 %copy-done = f32[12288,128]{1,0:T(8,128)S(1)} copy-done((f32[12288,128]{1,0:T(8,128)S(1)}, f32[12288,128]{1,0:T(8,128)}, u32[]{:S(2)}) %copy-start) | copy-done | bytes 6291480
  2.8 0.0 copy-start.2
  2.8 3.5 %gram.1 = f32[128,128]{1,0:T(8,128)S(1)} custom-call(f32[12288,128]{1,0:T(8,128)S(1)} %copy-done), custom_call_target="tpu_custom_call" | custom-call | tf_op jit(solution)/shard_map/gram/pallas_call | solution.py:139
  6.3 3.3 %collective-permute-start = (f32[128,128]{1,0:T(8,128)S(1)}, f32[128,128]{1,0:T(8,128)S(1)}, u32[]{:S(2)}, u32[]{:S(2)}) collective-permute-start(f32[128,128]{1,0:T(8,128)S(1)} %gram.1), channel_id=1, source_target_pairs={{0,16},{1,17},{2,18},{3,19},{4,20},{5,21},{6,22},{7,23},{8,24},{9,... | collective-permute-start | bytes 196616 | tf_op jit(solution)/shard_map/ppermute | solution.py:312
  9.6 0.9 collective-permute-done
  10.6 0.1 collective-permute-start.1
  10.7 3.1 %collective-permute-done.1 = f32[128,128]{1,0:T(8,128)S(1)} collective-permute-done((f32[128,128]{1,0:T(8,128)S(1)}, f32[128,128]{1,0:T(8,128)S(1)}, u32[]{:S(2)}, u32[]{:S(2)}) %collective-permute-start.1) | collective-permute-done | bytes 65568 | tf_op jit(solution)/shard_map/ppermute | solution.py:312
  13.8 1.9 %collective-permute-start.2 = (f32[128,128]{1,0:T(8,128)S(1)}, f32[128,128]{1,0:T(8,128)S(1)}, u32[]{:S(2)}, u32[]{:S(2)}) collective-permute-start(f32[128,128]{1,0:T(8,128)S(1)} %add.34), channel_id=1, source_target_pairs={{0,64},{1,65},{2,66},{3,67},{4,68},{5,69},{6,70},{7,71},{8,72},{9,... | collective-permute-start | bytes 196616 | tf_op jit(solution)/shard_map/ppermute | solution.py:312
  15.7 2.9 %collective-permute-done.2 = f32[128,128]{1,0:T(8,128)S(1)} collective-permute-done((f32[128,128]{1,0:T(8,128)S(1)}, f32[128,128]{1,0:T(8,128)S(1)}, u32[]{:S(2)}, u32[]{:S(2)}) %collective-permute-start.2) | collective-permute-done | bytes 65568 | tf_op jit(solution)/shard_map/ppermute | solution.py:312
  18.6 5.3 %collective-permute-start.3 = (f32[128,128]{1,0:T(8,128)S(1)}, f32[128,128]{1,0:T(8,128)S(1)}, u32[]{:S(2)}, u32[]{:S(2)}) collective-permute-start(f32[128,128]{1,0:T(8,128)S(1)} %add.35), channel_id=1, source_target_pairs={{0,128},{1,129},{2,130},{3,131},{4,132},{5,133},{6,134},{7,135},{8... | collective-permute-start | bytes 196616 | tf_op jit(solution)/shard_map/ppermute | solution.py:312
  23.9 0.0 copy-done.2
  23.9 0.6 dynamic_slice.3
  25.1 0.6 collective-permute-done.3
  25.7 12.9 %rotation.2.rows_ref = f32[128,128]{1,0:T(8,128)S(1)} custom-call(f32[128,128]{1,0:T(8,128)S(1)} %add.36.gram_ref), custom_call_target="tpu_custom_call" | custom-call | tf_op jit(solution)/shard_map/rotation/pallas_call | solution.py:110
  38.6 0.0 copy-start.1
  38.6 2.8 %copy-done.1 = f32[12288,128]{1,0:T(8,128)S(1)} copy-done((f32[12288,128]{1,0:T(8,128)S(1)}, f32[12288,128]{1,0:T(8,128)}, u32[]{:S(2)}) %copy-start.1) | copy-done | bytes 6291480
  41.4 3.7 %turn.1 = (f32[6144,128]{1,0:T(8,128)S(1)}, f32[6144,128]{1,0:T(8,128)S(1)}) custom-call(s32[1]{0:T(128)} %bitcast.1.flag_ref, f32[128,128]{1,0:T(8,128)S(1)} %rotation.2.rows_ref, f32[12288,128]{1,0:T(8,128)S(1)} %copy-done.1, f32[12288,128]{1,0:T(8,128)S(1)} %copy-done.1), custom_call_target="tpu_custom_call" | custom-call | tf_op jit(solution)/shard_map/turn/pallas_call | solution.py:180
  45.1 4.9 %collective-permute-start.4 = (f32[6144,128]{1,0:T(8,128)S(1)}, f32[6144,128]{1,0:T(8,128)S(1)}, u32[]{:S(2)}, u32[]{:S(2)}) collective-permute-start(f32[6144,128]{1,0:T(8,128)S(1)} %get-tuple-element.10.early_ref), channel_id=1, source_target_pairs={{0,1},{1,2},{2,3},{3,4},{4,5},{5,6},{6,7},{7,8},{8,9},{9,10},{10,1... | collective-permute-start | bytes 9437192 | tf_op jit(solution)/shard_map/ppermute | solution.py:312
  50.0 34.2 %collective-permute-done.4.come_ref = f32[6144,128]{1,0:T(8,128)S(1)} collective-permute-done((f32[6144,128]{1,0:T(8,128)S(1)}, f32[6144,128]{1,0:T(8,128)S(1)}, u32[]{:S(2)}, u32[]{:S(2)}) %collective-permute-start.4) | collective-permute-done | bytes 3145760 | tf_op jit(solution)/shard_map/ppermute | solution.py:312
  84.2 0.0 collective-permute-start.10
  84.2 3.2 %pair_gram.1 = f32[128,128]{1,0:T(8,128)S(1)} custom-call(s32[1]{0:T(128)} %bitcast.2.core_ref, f32[6144,128]{1,0:T(8,128)S(1)} %get-tuple-element.11.own_ref.late_ref, f32[6144,128]{1,0:T(8,128)S(1)} %collective-permute-done.4.come_ref), custom_call_target="tpu_custom_call" | custom-call | tf_op jit(solution)/shard_map/pair_gram/pallas_call | solution.py:232
  87.4 7.9 %collective-permute-start.5 = (f32[128,128]{1,0:T(8,128)S(1)}, f32[128,128]{1,0:T(8,128)S(1)}, u32[]{:S(2)}, u32[]{:S(2)}) collective-permute-start(f32[128,128]{1,0:T(8,128)S(1)} %pair_gram.1), channel_id=1, source_target_pairs={{0,31},{1,16},{2,17},{3,18},{4,19},{5,20},{6,21},{7,22},{8,23},{9,... | collective-permute-start | bytes 196616 | tf_op jit(solution)/shard_map/ppermute | solution.py:312
  95.4 32.2 %collective-permute-done.5 = f32[128,128]{1,0:T(8,128)S(1)} collective-permute-done((f32[128,128]{1,0:T(8,128)S(1)}, f32[128,128]{1,0:T(8,128)S(1)}, u32[]{:S(2)}, u32[]{:S(2)}) %collective-permute-start.5) | collective-permute-done | bytes 65568 | tf_op jit(solution)/shard_map/ppermute | solution.py:312
  127.6 0.1 collective-permute-start.6
  127.7 3.3 %collective-permute-done.6 = f32[128,128]{1,0:T(8,128)S(1)} collective-permute-done((f32[128,128]{1,0:T(8,128)S(1)}, f32[128,128]{1,0:T(8,128)S(1)}, u32[]{:S(2)}, u32[]{:S(2)}) %collective-permute-start.6) | collective-permute-done | bytes 65568 | tf_op jit(solution)/shard_map/ppermute | solution.py:312
  131.0 1.3 collective-permute-start.7
  132.4 4.7 %collective-permute-done.7 = f32[128,128]{1,0:T(8,128)S(1)} collective-permute-done((f32[128,128]{1,0:T(8,128)S(1)}, f32[128,128]{1,0:T(8,128)S(1)}, u32[]{:S(2)}, u32[]{:S(2)}) %collective-permute-start.7) | collective-permute-done | bytes 65568 | tf_op jit(solution)/shard_map/ppermute | solution.py:312
  137.0 3.5 %collective-permute-start.8 = (f32[128,128]{1,0:T(8,128)S(1)}, f32[128,128]{1,0:T(8,128)S(1)}, u32[]{:S(2)}, u32[]{:S(2)}) collective-permute-start(f32[128,128]{1,0:T(8,128)S(1)} %add.39), channel_id=1, source_target_pairs={{0,128},{1,129},{2,130},{3,131},{4,132},{5,133},{6,134},{7,135},{8... | collective-permute-start | bytes 196616 | tf_op jit(solution)/shard_map/ppermute | solution.py:312
  140.6 3.7 %collective-permute-done.8 = f32[128,128]{1,0:T(8,128)S(1)} collective-permute-done((f32[128,128]{1,0:T(8,128)S(1)}, f32[128,128]{1,0:T(8,128)S(1)}, u32[]{:S(2)}, u32[]{:S(2)}) %collective-permute-start.8) | collective-permute-done | bytes 65568 | tf_op jit(solution)/shard_map/ppermute | solution.py:312
  144.3 12.9 %rotation.3.mine_ref = f32[128,128]{1,0:T(8,128)S(1)} custom-call(f32[128,128]{1,0:T(8,128)S(1)} %add.40.gram_ref), custom_call_target="tpu_custom_call" | custom-call | tf_op jit(solution)/shard_map/rotation/pallas_call | solution.py:110
  157.2 2.6 %collective-permute-start.9 = (f32[128,128]{1,0:T(8,128)S(1)}, f32[128,128]{1,0:T(8,128)S(1)}, u32[]{:S(2)}, u32[]{:S(2)}) collective-permute-start(f32[128,128]{1,0:T(8,128)S(1)} %rotation.3.mine_ref), channel_id=1, source_target_pairs={{0,16},{1,17},{2,18},{3,19},{4,20},{5,21},{6,22},{7,23},{8,24},{9,... | collective-permute-start | bytes 196616 | tf_op jit(solution)/shard_map/ppermute | solution.py:312
  159.7 0.1 pad_add_fusion.flags_ref
  159.8 0.8 collective-permute-done.9.other_ref
  160.6 0.0 collective-permute-done.10.last_ref
  160.6 8.0 %finish.1 = f32[2,6144,128]{2,1,0:T(8,128)} custom-call(s32[2]{0:T(128)S(1)} %pad_add_fusion.flags_ref, f32[128,128]{1,0:T(8,128)S(1)} %rotation.3.mine_ref, f32[128,128]{1,0:T(8,128)S(1)} %collective-permute-done.9.other_ref, f32[6144,128]{1,0:T(8,128)S(1)} %get-tuple-element.10.early_ref, f32[6144,128]{1,0:T(8,128)S(1)} %get-tuple-element.11.own_ref.late_ref, ...), custom_call_target="tpu_custom_call" | custom-call | tf_op jit(solution)/shard_map/finish/pallas_call | solution.py:292
  (8 shorter events, 0.1 us)
Async XLA Ops:
  0.0 2.8 %copy-start = (f32[12288,128]{1,0:T(8,128)S(1)}, f32[12288,128]{1,0:T(8,128)}, u32[]{:S(2)}) copy-start(f32[12288,128]{1,0:T(8,128)} %bottom_ref.1) | copy-start | bytes 18874372
  2.8 21.1 %copy-start.2 = (s32[16]{0:T(128)S(1)}, s32[16]{0:T(128)}, u32[]{:S(2)}) copy-start(s32[16]{0:T(128)} %param.3) | copy-start | bytes 196
  6.3 4.2 %collective-permute-start = (f32[128,128]{1,0:T(8,128)S(1)}, f32[128,128]{1,0:T(8,128)S(1)}, u32[]{:S(2)}, u32[]{:S(2)}) collective-permute-start(f32[128,128]{1,0:T(8,128)S(1)} %gram.1), channel_id=1, source_target_pairs={{0,16},{1,17},{2,18},{3,19},{4,20},{5,21},{6,22},{7,23},{8,24},{9,... | collective-permute-start | bytes 196616 | tf_op jit(solution)/shard_map/ppermute | solution.py:312
  10.6 3.2 %collective-permute-start.1 = (f32[128,128]{1,0:T(8,128)S(1)}, f32[128,128]{1,0:T(8,128)S(1)}, u32[]{:S(2)}, u32[]{:S(2)}) collective-permute-start(f32[128,128]{1,0:T(8,128)S(1)} %add.33), channel_id=1, source_target_pairs={{0,32},{1,33},{2,34},{3,35},{4,36},{5,37},{6,38},{7,39},{8,40},{9,... | collective-permute-start | bytes 196616 | tf_op jit(solution)/shard_map/ppermute | solution.py:312
  13.8 4.8 %collective-permute-start.2 = (f32[128,128]{1,0:T(8,128)S(1)}, f32[128,128]{1,0:T(8,128)S(1)}, u32[]{:S(2)}, u32[]{:S(2)}) collective-permute-start(f32[128,128]{1,0:T(8,128)S(1)} %add.34), channel_id=1, source_target_pairs={{0,64},{1,65},{2,66},{3,67},{4,68},{5,69},{6,70},{7,71},{8,72},{9,... | collective-permute-start | bytes 196616 | tf_op jit(solution)/shard_map/ppermute | solution.py:312
  18.6 7.1 %collective-permute-start.3 = (f32[128,128]{1,0:T(8,128)S(1)}, f32[128,128]{1,0:T(8,128)S(1)}, u32[]{:S(2)}, u32[]{:S(2)}) collective-permute-start(f32[128,128]{1,0:T(8,128)S(1)} %add.35), channel_id=1, source_target_pairs={{0,128},{1,129},{2,130},{3,131},{4,132},{5,133},{6,134},{7,135},{8... | collective-permute-start | bytes 196616 | tf_op jit(solution)/shard_map/ppermute | solution.py:312
  38.6 2.8 %copy-start.1 = (f32[12288,128]{1,0:T(8,128)S(1)}, f32[12288,128]{1,0:T(8,128)}, u32[]{:S(2)}) copy-start(f32[12288,128]{1,0:T(8,128)} %bottom_ref.1) | copy-start | bytes 18874372
  45.1 39.1 %collective-permute-start.4 = (f32[6144,128]{1,0:T(8,128)S(1)}, f32[6144,128]{1,0:T(8,128)S(1)}, u32[]{:S(2)}, u32[]{:S(2)}) collective-permute-start(f32[6144,128]{1,0:T(8,128)S(1)} %get-tuple-element.10.early_ref), channel_id=1, source_target_pairs={{0,1},{1,2},{2,3},{3,4},{4,5},{5,6},{6,7},{7,8},{8,9},{9,10},{10,1... | collective-permute-start | bytes 9437192 | tf_op jit(solution)/shard_map/ppermute | solution.py:312
  84.2 76.4 %collective-permute-start.10 = (f32[6144,128]{1,0:T(8,128)S(1)}, f32[6144,128]{1,0:T(8,128)S(1)}, u32[]{:S(2)}, u32[]{:S(2)}) collective-permute-start(f32[6144,128]{1,0:T(8,128)S(1)} %get-tuple-element.11.own_ref.late_ref), channel_id=1, source_target_pairs={{0,15},{1,0},{2,1},{3,2},{4,3},{5,4},{6,5},{7,6},{8,7},{9,8},{10,9... | collective-permute-start | bytes 9437192 | tf_op jit(solution)/shard_map/ppermute | solution.py:312
  87.4 40.1 %collective-permute-start.5 = (f32[128,128]{1,0:T(8,128)S(1)}, f32[128,128]{1,0:T(8,128)S(1)}, u32[]{:S(2)}, u32[]{:S(2)}) collective-permute-start(f32[128,128]{1,0:T(8,128)S(1)} %pair_gram.1), channel_id=1, source_target_pairs={{0,31},{1,16},{2,17},{3,18},{4,19},{5,20},{6,21},{7,22},{8,23},{9,... | collective-permute-start | bytes 196616 | tf_op jit(solution)/shard_map/ppermute | solution.py:312
  127.6 3.4 %collective-permute-start.6 = (f32[128,128]{1,0:T(8,128)S(1)}, f32[128,128]{1,0:T(8,128)S(1)}, u32[]{:S(2)}, u32[]{:S(2)}) collective-permute-start(f32[128,128]{1,0:T(8,128)S(1)} %add.37), channel_id=1, source_target_pairs={{0,32},{1,33},{2,34},{3,35},{4,36},{5,37},{6,38},{7,39},{8,40},{9,... | collective-permute-start | bytes 196616 | tf_op jit(solution)/shard_map/ppermute | solution.py:312
  131.0 6.0 %collective-permute-start.7 = (f32[128,128]{1,0:T(8,128)S(1)}, f32[128,128]{1,0:T(8,128)S(1)}, u32[]{:S(2)}, u32[]{:S(2)}) collective-permute-start(f32[128,128]{1,0:T(8,128)S(1)} %add.38), channel_id=1, source_target_pairs={{0,64},{1,65},{2,66},{3,67},{4,68},{5,69},{6,70},{7,71},{8,72},{9,... | collective-permute-start | bytes 196616 | tf_op jit(solution)/shard_map/ppermute | solution.py:312
  137.0 7.2 %collective-permute-start.8 = (f32[128,128]{1,0:T(8,128)S(1)}, f32[128,128]{1,0:T(8,128)S(1)}, u32[]{:S(2)}, u32[]{:S(2)}) collective-permute-start(f32[128,128]{1,0:T(8,128)S(1)} %add.39), channel_id=1, source_target_pairs={{0,128},{1,129},{2,130},{3,131},{4,132},{5,133},{6,134},{7,135},{8... | collective-permute-start | bytes 196616 | tf_op jit(solution)/shard_map/ppermute | solution.py:312
  157.2 3.5 %collective-permute-start.9 = (f32[128,128]{1,0:T(8,128)S(1)}, f32[128,128]{1,0:T(8,128)S(1)}, u32[]{:S(2)}, u32[]{:S(2)}) collective-permute-start(f32[128,128]{1,0:T(8,128)S(1)} %rotation.3.mine_ref), channel_id=1, source_target_pairs={{0,16},{1,17},{2,18},{3,19},{4,20},{5,21},{6,22},{7,23},{8,24},{9,... | collective-permute-start | bytes 196616 | tf_op jit(solution)/shard_map/ppermute | solution.py:312

commit v2 on v1

v2 whole, which is shorter than its diff:
```python
import functools

import jax
import jax.numpy as jnp
from jax import lax
from jax.experimental import pallas as pl
from jax.experimental.pallas import tpu as pltpu
from jax.sharding import PartitionSpec as P

ITERS = 3
ORDER = 128
HALF = 64
GROUP = 8
TILE = 512
RAW_TILES = 6
GRAM_LIMIT = 48
F32 = jnp.float32
BF16 = jnp.bfloat16


def split_two(value):
    high = value.astype(BF16)
    low = (value - high.astype(F32)).astype(BF16)
    return high, low


def split_three(value):
    high = value.astype(BF16)
    rest = value - high.astype(F32)
    middle = rest.astype(BF16)
    low = (rest - middle.astype(F32)).astype(BF16)
    return high, middle, low


def dot_bf16(left, right, dims):
    return lax.dot_general(left, right, (dims, ((), ())), preferred_element_type=F32)


def dot_six(left, right, transpose_right):
    lh, lm, ll = split_three(left)
    rh, rm, rl = split_three(right)
    axis = 1 if transpose_right else 0
    dims = ((1,), (axis,))
    total = None
    for (la, ra), (lb, rb) in (((lh, rl), (ll, rh)), ((lm, rm), (lm, rh)), ((lh, rm), (lh, rh))):
        term = dot_bf16(
            jnp.concatenate([la, lb], axis=1), jnp.concatenate([ra, rb], axis=axis), dims
        )
        total = term if total is None else total + term
    return total


def across(column, rows):
    return jnp.broadcast_to(column, (rows, ORDER))


def orthonormal_rows(normal, rows_in):
    done = []
    spot = lax.broadcasted_iota(jnp.int32, (GROUP, ORDER), 0)
    for start in range(0, ORDER, GROUP):
        tail = ORDER - start - GROUP
        head_n, head_y = normal[:GROUP], rows_in[:GROUP]
        tail_n, tail_y = normal[GROUP:], rows_in[GROUP:]
        head_c = [across(head_n[:, start + j : start + j + 1], GROUP) for j in range(GROUP)]
        tail_c = [across(tail_n[:, start + j : start + j + 1], tail) for j in range(GROUP)] if tail else []
        pivots = head_c[0]
        for k in range(GROUP):
            pivot = across(head_c[k][k : k + 1], GROUP)
            inverse = 1.0 / pivot
            row_n = head_n[k : k + 1]
            row_y = head_y[k : k + 1]
            if k:
                pivots = jnp.where(spot >= k, pivot, pivots)
            else:
                pivots = pivot
            cross = [head_c[j][k : k + 1] for j in range(k + 1, GROUP)]
            if k < GROUP - 1:
                scaled = jnp.where(spot > k, head_c[k] * inverse, 0.0)
                head_n = head_n - scaled * row_n
                head_y = head_y - scaled * row_y
                for j in range(k + 1, GROUP):
                    head_c[j] = head_c[j] - scaled * cross[j - k - 1]
            if tail:
                scaled = tail_c[k] * inverse[:1]
                tail_n = tail_n - scaled * row_n
                tail_y = tail_y - scaled * row_y
                for j in range(k + 1, GROUP):
                    tail_c[j] = tail_c[j] - scaled * cross[j - k - 1]
        done.append(head_y * lax.rsqrt(pivots))
        normal, rows_in = tail_n, tail_y
    return jnp.concatenate(done, axis=0)


def rotation_kernel(flag_ref, gram_ref, out_ref, half_ref):
    gram = gram_ref[...]
    gram = gram * (1.0 / jnp.max(jnp.abs(gram)))

    def turn(rows):
        out_ref[...] = orthonormal_rows(dot_six(rows, rows, True), rows)

    turn(gram)

    def step(_, carry):
        turn(dot_six(out_ref[...], gram, False))
        return carry

    lax.fori_loop(1, ITERS, step, 0)
    half_ref[...] = jnp.where(flag_ref[0] == 1, out_ref[:HALF], out_ref[HALF:])


def rotation_rows(flag, gram_total):
    vmem = pl.BlockSpec(memory_space=pltpu.VMEM)
    return pl.pallas_call(
        rotation_kernel,
        out_shape=(
            jax.ShapeDtypeStruct((ORDER, ORDER), F32),
            jax.ShapeDtypeStruct((HALF, ORDER), F32),
        ),
        in_specs=[pl.BlockSpec(memory_space=pltpu.SMEM), vmem],
        out_specs=(vmem, vmem),
        compiler_params=limit(8),
        name="rotation",
    )(flag, gram_total)


def vmem():
    return pl.BlockSpec(memory_space=pltpu.VMEM)


def smem():
    return pl.BlockSpec(memory_space=pltpu.SMEM)


def limit(megabytes):
    return pltpu.CompilerParams(vmem_limit_bytes=megabytes * 2**20)


def tile_rows(tile, size):
    return pl.ds(pl.multiple_of(tile * size, size), size)


def gram_kernel(x_ref, out_ref, sent_ref, rest_ref, held, sems, sent_sems):
    size = 2 * TILE
    places, copies, sends = [], [], []
    for tile in range(x_ref.shape[0] // size):
        rows = pl.ds(tile * size, size)
        place = held.at[rows] if tile < RAW_TILES else rest_ref.at[pl.ds((tile - RAW_TILES) * size, size)]
        places.append(place)
        copies.append(pltpu.make_async_copy(x_ref.at[rows], place, sems.at[tile]))
        if tile < RAW_TILES:
            sends.append(pltpu.make_async_copy(place, sent_ref.at[rows], sent_sems.at[tile]))
    for copy in copies:
        copy.start()
    total = jnp.zeros((ORDER, 2 * ORDER), F32)
    for tile, copy in enumerate(copies):
        copy.wait()
        if tile < RAW_TILES:
            sends[tile].start()
        high, low = split_two(places[tile][...])
        total = total + dot_bf16(high, jnp.concatenate([high, low], axis=1), ((0,), (0,)))
    mixed = total[:, ORDER:]
    out_ref[...] = total[:, :ORDER] + (mixed + mixed.T)
    for send in sends:
        send.wait()


def gram_and_rows(columns):
    rows = columns.shape[0]
    tiles = rows // (2 * TILE)
    raw_rows = RAW_TILES * 2 * TILE
    return pl.pallas_call(
        gram_kernel,
        out_shape=(
            jax.ShapeDtypeStruct((ORDER, ORDER), F32),
            jax.ShapeDtypeStruct((raw_rows, ORDER), F32),
            jax.ShapeDtypeStruct((rows - raw_rows, ORDER), F32),
        ),
        in_specs=[pl.BlockSpec(memory_space=pl.ANY)],
        out_specs=(vmem(), pl.BlockSpec(memory_space=pl.ANY), vmem()),
        scratch_shapes=[
            pltpu.VMEM((raw_rows, ORDER), F32),
            pltpu.SemaphoreType.DMA((tiles,)),
            pltpu.SemaphoreType.DMA((RAW_TILES,)),
        ],
        compiler_params=limit(GRAM_LIMIT),
        name="gram",
    )(columns)


def store_weights(weights, high, low):
    high[...], low[...] = split_two(weights)


def dot_three(value, high, low):
    value_high, value_low = split_two(value)
    dims = ((1,), (0,))
    width = high.shape[1]
    if width > ORDER:
        small = dot_bf16(value_high, low[...], dims) + dot_bf16(value_low, high[...], dims)
        return dot_bf16(value_high, high[...], dims) + small
    both = dot_bf16(value_high, jnp.concatenate([high[...], low[...]], axis=1), dims)
    return both[:, :width] + (both[:, width:] + dot_bf16(value_low, high[...], dims))


def packed(ref, tile):
    return jnp.concatenate([ref[tile_rows(2 * tile, TILE)], ref[tile_rows(2 * tile + 1, TILE)]], axis=1)


def turn_kernel(flag_ref, rows_ref, x_ref, early_ref, late_ref, high, low):
    front, back = rows_ref[:HALF], rows_ref[HALF:]
    is_back = flag_ref[0] == 1
    early = jnp.where(is_back, back, front)
    late = jnp.where(is_back, front, back)
    none = jnp.zeros_like(early)
    upper = jnp.concatenate([early, none, late, none], axis=0)
    lower = jnp.concatenate([none, early, none, late], axis=0)
    store_weights(jnp.concatenate([upper, lower], axis=1).T, high, low)

    @pl.loop(0, early_ref.shape[0] // TILE)
    def _(tile):
        out = dot_three(packed(x_ref, tile), high, low)
        early_ref[tile_rows(tile, TILE)] = out[:, :ORDER]
        late_ref[tile_rows(tile, TILE)] = out[:, ORDER:]


def turn(columns, turn_rows, early_is_back):
    half = jax.ShapeDtypeStruct((columns.shape[0] // 2, ORDER), F32)
    return pl.pallas_call(
        turn_kernel,
        out_shape=(half, half),
        in_specs=[smem(), vmem(), vmem()],
        out_specs=(vmem(), vmem()),
        scratch_shapes=[pltpu.VMEM((2 * ORDER, 2 * ORDER), BF16)] * 2,
        compiler_params=limit(16),
        name="turn",
    )(early_is_back, turn_rows, columns)


def turn_raw_kernel(rows_ref, x_ref, out_ref, high, low):
    rows = rows_ref[...]
    none = jnp.zeros_like(rows)
    upper = jnp.concatenate([rows, none], axis=0)
    lower = jnp.concatenate([none, rows], axis=0)
    store_weights(jnp.concatenate([upper, lower], axis=1).T, high, low)

    @pl.loop(0, out_ref.shape[0] // TILE)
    def _(tile):
        out_ref[tile_rows(tile, TILE)] = dot_three(packed(x_ref, tile), high, low)


def turn_raw(columns, half_rows):
    return pl.pallas_call(
        turn_raw_kernel,
        out_shape=jax.ShapeDtypeStruct((columns.shape[0] // 2, ORDER), F32),
        in_specs=[vmem(), vmem()],
        out_specs=vmem(),
        scratch_shapes=[pltpu.VMEM((2 * ORDER, ORDER), BF16)] * 2,
        compiler_params=limit(16),
        name="turn_raw",
    )(half_rows, columns)


def half_roll(value, axis):
    return pltpu.roll(value, HALF, axis)


def low_lanes(shape):
    return lax.broadcasted_iota(jnp.int32, shape, 1) < HALF


def pair_gram_kernel(core_ref, before_ref, own_ref, come_ref, out_ref, total):
    total[...] = jnp.zeros_like(total)

    @pl.loop(0, own_ref.shape[0] // TILE)
    def _(tile):
        rows = tile_rows(tile, TILE)
        high, low = split_two(jnp.concatenate([own_ref[rows], come_ref[rows]], axis=1))
        total[...] += dot_bf16(high, jnp.concatenate([high, low], axis=1), ((0,), (0,)))

    mixed = total[:, 2 * ORDER :]
    whole = total[:, : 2 * ORDER] + (mixed + mixed.T)
    tops = jnp.concatenate([whole[:HALF], whole[ORDER : ORDER + HALF]], axis=0)
    bottoms = jnp.concatenate([whole[HALF:ORDER], whole[ORDER + HALF :]], axis=0)
    first = low_lanes((ORDER, ORDER))
    gram = jnp.where(first, tops[:, :ORDER], half_roll(tops[:, ORDER:], 1)) + jnp.where(
        first, half_roll(bottoms[:, :ORDER], 1), bottoms[:, ORDER:]
    )
    swapped = half_roll(half_roll(gram, 1), 0)
    out_ref[...] = before_ref[...] + jnp.where(core_ref[0] == 1, swapped, gram)


def pair_gram(core, before, own, come):
    return pl.pallas_call(
        pair_gram_kernel,
        out_shape=jax.ShapeDtypeStruct((ORDER, ORDER), F32),
        in_specs=[smem(), vmem(), vmem(), vmem()],
        out_specs=vmem(),
        scratch_shapes=[pltpu.VMEM((2 * ORDER, 4 * ORDER), F32)],
        compiler_params=limit(16),
        name="pair_gram",
    )(core, before, own, come)


def finish_kernel(places, flags_ref, mine_ref, other_ref, *refs):
    parts, (out_ref, early_high, early_low, late_high, late_low, held, sems) = refs[:-7], refs[-7:]
    swap = flags_ref[1] == 1

    def ordered(rows):
        return jnp.where(swap, half_roll(half_roll(rows, 1), 0), rows)

    first = low_lanes((HALF, ORDER))
    late_rows = ordered(mine_ref[...])[:HALF]
    early_rows = ordered(other_ref[...])[HALF:]
    late_own, late_come = jnp.where(first, late_rows, 0.0), jnp.where(first, 0.0, late_rows)
    early_last, early_own = jnp.where(first, early_rows, 0.0), jnp.where(first, 0.0, early_rows)

    def store(upper, lower, lower_first, high, low):
        above = jnp.where(lower_first, lower, upper)
        below = jnp.where(lower_first, upper, lower)
        store_weights(jnp.concatenate([above, below], axis=0).T, high, low)

    is_back = flags_ref[0] == 1
    store(
        jnp.concatenate([half_roll(early_own, 1), early_last], axis=1),
        jnp.concatenate([early_own, half_roll(early_last, 1)], axis=1),
        is_back,
        early_high,
        early_low,
    )
    store(
        jnp.concatenate([late_own, half_roll(late_come, 1)], axis=1),
        jnp.concatenate([half_roll(late_own, 1), late_come], axis=1),
        jnp.logical_not(is_back),
        late_high,
        late_low,
    )
    late_lanes = low_lanes((TILE, ORDER)) == is_back

    def out_copy(tile):
        size = 2 * TILE
        return pltpu.make_async_copy(held.at[tile], out_ref.at[tile_rows(tile, size)], sems.at[tile])

    for index, (place, tiles) in enumerate(places):
        early_ref, late_ref, come_ref, last_ref = parts[4 * index : 4 * index + 4]

        @pl.loop(0, tiles)
        def _(tile):
            rows = tile_rows(tile, TILE)
            early = jnp.concatenate([early_ref[rows], last_ref[rows]], axis=1)
            late = jnp.concatenate([late_ref[rows], come_ref[rows]], axis=1)
            early = dot_three(early, early_high, early_low)
            late = dot_three(late, late_high, late_low)
            held[tile + place, :TILE] = jnp.where(late_lanes, late, early)
            held[tile + place, TILE:] = half_roll(jnp.where(late_lanes, early, late), 1)
            out_copy(tile + place).start()

    for tile in range(held.shape[0]):
        out_copy(tile).wait()


def finish(flags, mine, other, places, parts, rows):
    tiles = rows // (2 * TILE)
    return pl.pallas_call(
        functools.partial(finish_kernel, places),
        out_shape=jax.ShapeDtypeStruct((rows, ORDER), F32),
        in_specs=[smem()] + [vmem()] * (2 + len(parts)),
        out_specs=pl.BlockSpec(memory_space=pl.ANY),
        scratch_shapes=[
            pltpu.VMEM((2 * ORDER, ORDER), BF16),
            pltpu.VMEM((2 * ORDER, ORDER), BF16),
            pltpu.VMEM((2 * ORDER, ORDER), BF16),
            pltpu.VMEM((2 * ORDER, ORDER), BF16),
            pltpu.VMEM((tiles, 2 * TILE, ORDER), F32),
            pltpu.SemaphoreType.DMA((tiles,)),
        ],
        compiler_params=limit(24),
        name="finish",
    )(flags, mine, other, *parts)


def moved(array, target):
    rows, cols = lax.axis_size("row"), lax.axis_size("col")
    pairs = []
    for row in range(rows):
        for col in range(cols):
            to_row, to_col = target(row, col)
            pairs.append((row * cols + col, (to_row % rows) * cols + to_col % cols))
    return lax.ppermute(array, ("row", "col"), pairs)


def outward(row, col):
    return row, col + (1 if row % 2 == 0 else -1)


def inward(row, col):
    return row, col + (-1 if row % 2 == 0 else 1)


def inward_swapped(row, col):
    to_row, to_col = inward(row, col)
    return to_row ^ 1, to_col


def swap_rows(by):
    return lambda row, col: (row ^ by, col)


def summed(gram):
    for by in (2, 4, 8):
        gram = gram + moved(gram, swap_rows(by))
    return gram


def tied(first, *others):
    return lax.optimization_barrier((first, *others))[0]


def local(matrix, plan):
    rows = matrix.shape[0]
    tiles = rows // (2 * TILE)
    core = lax.axis_index("row") % 2
    leaver = plan[lax.axis_index("col")]
    early_is_back = leaver ^ core
    flag, core_flag = early_is_back.reshape(1), core.reshape(1)
    rest_tiles = tiles - RAW_TILES
    places = ((0, RAW_TILES), (RAW_TILES, rest_tiles))

    gram, sent, rest = gram_and_rows(matrix)
    raw_come = moved(sent, outward)
    gram = gram + moved(gram, swap_rows(1))
    first_turn, half_turn = rotation_rows(flag, summed(gram))
    come_turn = moved(half_turn, inward_swapped)

    early_b, late_b = turn(rest, first_turn, flag)
    come_b = moved(early_b, outward)
    early_a, late_a = turn(sent, tied(first_turn, early_b, come_turn), flag)
    come_a = turn_raw(raw_come, come_turn)
    second = pair_gram(core_flag, jnp.zeros_like(gram), late_a, come_a)
    second = pair_gram(core_flag, second, late_b, come_b)
    last_a = moved(tied(late_a, come_b), inward)
    last_b = moved(tied(late_b, come_b, come_turn), inward)
    second = second + moved(moved(second, swap_rows(1)), outward)
    mine, _ = rotation_rows(flag, summed(second))
    other = moved(mine, swap_rows(1))
    flags = jnp.stack([early_is_back, core])
    parts = [early_a, late_a, come_a, last_a, early_b, late_b, come_b, last_b]
    return finish(flags, mine, other, places, parts, rows)


def solution(mesh):
    in_specs = (P("row", "col"), P())
    out_specs = P("row", "col")
    return jax.shard_map(local, mesh=mesh, in_specs=in_specs, out_specs=out_specs, check_vma=False)
```

time: 169 us -> 134 us (0.79)
  waiting for transfers between devices: 86.4 us -> 30.9 us
  starting transfers between devices: 31 us -> 45 us
  Pallas kernels: 44.2 us -> 53.9 us
  local copies, waits for them, and re-layouts: 6.19 us -> 2.48 us
    ppermute x11 -> x15, waiting for transfers between devices: 86.4 us -> 30.9 us  [moved(): return lax.ppermute(array, ('row', 'col'), pairs)]
    ppermute x11 -> x15, starting transfers between devices: 31 us -> 45 us  [moved(): return lax.ppermute(array, ('row', 'col'), pairs)]
    pallas_call x6 -> x9, Pallas kernels: 44.2 us -> 53.9 us  [the longest x2 26.4 us: rotation_rows(): pl.pallas_call(rotation_kernel, out_shape=(jax.ShapeDtypeStruct((ORDER, O...]
    unnamed x6 -> x4, local copies, waits for them, and re-layouts: 5.58 us -> 1.9 us
  transfers between devices with their start and end apart: 11 -> 15, of which waited for: 10 -> 12; matrix products, arithmetic and copies ran while one was open for 0% -> 1% of each run, Pallas kernels for 10% -> 30%
where the time goes in v2:
time: 134 us; the launch traced here: 133 us
  Pallas kernels  53.9 us (40%)
  starting transfers between devices  45 us (34%)
  waiting for transfers between devices  30.9 us (23%)
  local copies, waits for them, and re-layouts  2.48 us (2%)
    ppermute x15, starting transfers between devices, moved(): return lax.ppermute(array, ('row', 'col'), pairs)  45 us
    ppermute x15, waiting for transfers between devices, moved(): return lax.ppermute(array, ('row', 'col'), pairs)  30.9 us
    pallas_call x2, Pallas kernels, rotation_rows(): pl.pallas_call(rotation_kernel, out_shape=(jax.ShapeDtypeStruct((ORDER, O...  26.4 us
    pallas_call x1, Pallas kernels, finish(): pl.pallas_call(functools.partial(finish_kernel, places), out_shape=jax.Sh...  8.02 us
    pallas_call x2, Pallas kernels, turn(): pl.pallas_call(turn_kernel, out_shape=(half, half), in_specs=[smem(), vme...  6.68 us
    pallas_call x1, Pallas kernels, gram_and_rows(): pl.pallas_call(gram_kernel, out_shape=(jax.ShapeDtypeStruct((ORDER, ORDER...  6.18 us
    pallas_call x2, Pallas kernels, pair_gram(): pl.pallas_call(pair_gram_kernel, out_shape=jax.ShapeDtypeStruct((ORDER, O...  4.53 us
  transfers between devices with their start and end apart: 15, of which 12 were waited for; matrix products, arithmetic and copies ran while one was open for 1% of the time, Pallas kernels for 30%

profile of v2, /device:TPU:1, one launch (start us, length us, event | category | flops | bytes accessed | tf_op | source)
XLA Modules:
  0.0 133.4 jit_solution(8639670844981389711)
XLA Ops:
  0.0 0.0 copy-start.1
  0.0 6.2 %gram.1 = (f32[128,128]{1,0:T(8,128)S(1)}, f32[6144,128]{1,0:T(8,128)}, f32[6144,128]{1,0:T(8,128)}) custom-call(f32[12288,128]{1,0:T(8,128)} %x_ref.1), custom_call_target="tpu_custom_call" | custom-call | tf_op jit(solution)/shard_map/gram/pallas_call | solution.py:171
  6.2 5.8 %collective-permute-start.5 = (f32[6144,128]{1,0:T(8,128)}, f32[6144,128]{1,0:T(8,128)S(1)}, u32[]{:S(2)}, u32[]{:S(2)}) collective-permute-start(f32[6144,128]{1,0:T(8,128)} %get-tuple-element.24.x_ref), channel_id=1, source_target_pairs={{0,1},{1,2},{2,3},{3,4},{4,5},{5,6},{6,7},{7,8},{8,9},{9,10},{10,1... | collective-permute-start | bytes 9437192 | tf_op jit(solution)/shard_map/ppermute | solution.py:388
  12.0 0.0 collective-permute-start
  12.0 1.3 collective-permute-done
  13.3 1.7 %collective-permute-start.1 = (f32[128,128]{1,0:T(8,128)S(1)}, f32[128,128]{1,0:T(8,128)S(1)}, u32[]{:S(2)}, u32[]{:S(2)}) collective-permute-start(f32[128,128]{1,0:T(8,128)S(1)} %add.33), channel_id=1, source_target_pairs={{0,32},{1,33},{2,34},{3,35},{4,36},{5,37},{6,38},{7,39},{8,40},{9,... | collective-permute-start | bytes 196616 | tf_op jit(solution)/shard_map/ppermute | solution.py:388
  15.0 2.3 %collective-permute-done.1 = f32[128,128]{1,0:T(8,128)S(1)} collective-permute-done((f32[128,128]{1,0:T(8,128)S(1)}, f32[128,128]{1,0:T(8,128)S(1)}, u32[]{:S(2)}, u32[]{:S(2)}) %collective-permute-start.1) | collective-permute-done | bytes 65568 | tf_op jit(solution)/shard_map/ppermute | solution.py:388
  17.3 3.1 %collective-permute-start.2 = (f32[128,128]{1,0:T(8,128)S(1)}, f32[128,128]{1,0:T(8,128)S(1)}, u32[]{:S(2)}, u32[]{:S(2)}) collective-permute-start(f32[128,128]{1,0:T(8,128)S(1)} %add.34), channel_id=1, source_target_pairs={{0,64},{1,65},{2,66},{3,67},{4,68},{5,69},{6,70},{7,71},{8,72},{9,... | collective-permute-start | bytes 196616 | tf_op jit(solution)/shard_map/ppermute | solution.py:388
  20.4 2.0 %collective-permute-done.2 = f32[128,128]{1,0:T(8,128)S(1)} collective-permute-done((f32[128,128]{1,0:T(8,128)S(1)}, f32[128,128]{1,0:T(8,128)S(1)}, u32[]{:S(2)}, u32[]{:S(2)}) %collective-permute-start.2) | collective-permute-done | bytes 65568 | tf_op jit(solution)/shard_map/ppermute | solution.py:388
  22.4 6.9 %collective-permute-start.3 = (f32[128,128]{1,0:T(8,128)S(1)}, f32[128,128]{1,0:T(8,128)S(1)}, u32[]{:S(2)}, u32[]{:S(2)}) collective-permute-start(f32[128,128]{1,0:T(8,128)S(1)} %add.35), channel_id=1, source_target_pairs={{0,128},{1,129},{2,130},{3,131},{4,132},{5,133},{6,134},{7,135},{8... | collective-permute-start | bytes 196616 | tf_op jit(solution)/shard_map/ppermute | solution.py:388
  29.2 0.0 copy-done.1
  29.2 0.6 dynamic_slice.3
  30.4 0.5 collective-permute-done.3
  30.9 12.9 %rotation.2 = (f32[128,128]{1,0:T(8,128)S(1)}, f32[64,128]{1,0:T(8,128)S(1)}) custom-call(s32[1]{0:T(128)} %bitcast.1.flag_ref, f32[128,128]{1,0:T(8,128)S(1)} %add.36.gram_ref), custom_call_target="tpu_custom_call" | custom-call | tf_op jit(solution)/shard_map/rotation/pallas_call | solution.py:113
  43.8 0.0 copy-start
  43.8 1.9 %copy-done = f32[6144,128]{1,0:T(8,128)S(1)} copy-done((f32[6144,128]{1,0:T(8,128)S(1)}, f32[6144,128]{1,0:T(8,128)}, u32[]{:S(2)}) %copy-start) | copy-done | bytes 3145752
  45.7 2.4 %turn.2 = (f32[3072,128]{1,0:T(8,128)S(1)}, f32[3072,128]{1,0:T(8,128)S(1)}) custom-call(s32[1]{0:T(128)} %bitcast.1.flag_ref, f32[128,128]{1,0:T(8,128)S(1)} %get-tuple-element.23.rows_ref, f32[6144,128]{1,0:T(8,128)S(1)} %copy-done), custom_call_target="tpu_custom_call" | custom-call | tf_op jit(solution)/shard_map/turn/pallas_call | solution.py:228
  48.1 0.3 collective-permute-start.6
  48.4 1.9 %collective-permute-start.4 = (f32[64,128]{1,0:T(8,128)S(1)}, f32[64,128]{1,0:T(8,128)S(1)}, u32[]{:S(2)}, u32[]{:S(2)}) collective-permute-start(f32[64,128]{1,0:T(8,128)S(1)} %get-tuple-element.22), channel_id=1, source_target_pairs={{0,31},{1,16},{2,17},{3,18},{4,19},{5,20},{6,21},{7,22},{8,23},{9,... | collective-permute-start | bytes 98312 | tf_op jit(solution)/shard_map/ppermute | solution.py:388
  50.3 1.9 %collective-permute-done.4.rows_ref = f32[64,128]{1,0:T(8,128)S(1)} collective-permute-done((f32[64,128]{1,0:T(8,128)S(1)}, f32[64,128]{1,0:T(8,128)S(1)}, u32[]{:S(2)}, u32[]{:S(2)}) %collective-permute-start.4) | collective-permute-done | bytes 32800 | tf_op jit(solution)/shard_map/ppermute | solution.py:388
  52.2 4.3 %turn.3 = (f32[3072,128]{1,0:T(8,128)S(1)}, f32[3072,128]{1,0:T(8,128)S(1)}) custom-call(s32[1]{0:T(128)} %bitcast.1.flag_ref, f32[128,128]{1,0:T(8,128)S(1)} %get-tuple-element.23.rows_ref, f32[6144,128]{1,0:T(8,128)} %get-tuple-element.24.x_ref), custom_call_target="tpu_custom_call" | custom-call | tf_op jit(solution)/shard_map/turn/pallas_call | solution.py:228
  56.5 11.6 %collective-permute-done.6.come_ref.refs_6_ = f32[3072,128]{1,0:T(8,128)S(1)} collective-permute-done((f32[3072,128]{1,0:T(8,128)S(1)}, f32[3072,128]{1,0:T(8,128)S(1)}, u32[]{:S(2)}, u32[]{:S(2)}) %collective-permute-start.6) | collective-permute-done | bytes 1572896 | tf_op jit(solution)/shard_map/ppermute | solution.py:388
  68.1 0.0 collective-permute-start.14
  68.1 0.0 collective-permute-start.13
  68.1 0.0 collective-permute-done.5.x_ref
  68.1 2.0 %turn_raw.1.come_ref.refs_2_ = f32[3072,128]{1,0:T(8,128)S(1)} custom-call(f32[64,128]{1,0:T(8,128)S(1)} %collective-permute-done.4.rows_ref, f32[6144,128]{1,0:T(8,128)S(1)} %collective-permute-done.5.x_ref), custom_call_target="tpu_custom_call" | custom-call | tf_op jit(solution)/shard_map/turn_raw/pallas_call | solution.py:252
  70.2 2.3 %pair_gram.2.before_ref = f32[128,128]{1,0:T(8,128)S(1)} custom-call(s32[1]{0:T(128)} %bitcast.2.core_ref, f32[128,128]{1,0:T(8,128)S(1)} %broadcast_in_dim.3.before_ref, f32[3072,128]{1,0:T(8,128)S(1)} %get-tuple-element.29.own_ref.refs_1_, f32[3072,128]{1,0:T(8,128)S(1)} %turn_raw.1.come_ref.refs_2_), custom_call_target="tpu_custom_call" | custom-call | tf_op jit(solution)/shard_map/pair_gram/pallas_call | solution.py:293
  72.5 2.3 %pair_gram.3 = f32[128,128]{1,0:T(8,128)S(1)} custom-call(s32[1]{0:T(128)} %bitcast.2.core_ref, f32[128,128]{1,0:T(8,128)S(1)} %pair_gram.2.before_ref, f32[3072,128]{1,0:T(8,128)S(1)} %get-tuple-element.30.own_ref.refs_5_, f32[3072,128]{1,0:T(8,128)S(1)} %collective-permute-done.6.come_ref.refs_6_), custom_call_target="tpu_custom_call" | custom-call | tf_op jit(solution)/shard_map/pair_gram/pallas_call | solution.py:293
  74.7 7.3 %collective-permute-start.7 = (f32[128,128]{1,0:T(8,128)S(1)}, f32[128,128]{1,0:T(8,128)S(1)}, u32[]{:S(2)}, u32[]{:S(2)}) collective-permute-start(f32[128,128]{1,0:T(8,128)S(1)} %pair_gram.3), channel_id=1, source_target_pairs={{0,16},{1,17},{2,18},{3,19},{4,20},{5,21},{6,22},{7,23},{8,24},{9,... | collective-permute-start | bytes 196616 | tf_op jit(solution)/shard_map/ppermute | solution.py:388
  82.0 0.9 collective-permute-done.7
  82.9 0.7 collective-permute-start.8
  83.6 3.5 %collective-permute-done.8 = f32[128,128]{1,0:T(8,128)S(1)} collective-permute-done((f32[128,128]{1,0:T(8,128)S(1)}, f32[128,128]{1,0:T(8,128)S(1)}, u32[]{:S(2)}, u32[]{:S(2)}) %collective-permute-start.8) | collective-permute-done | bytes 65568 | tf_op jit(solution)/shard_map/ppermute | solution.py:388
  87.1 0.7 collective-permute-start.9
  87.8 2.8 %collective-permute-done.9 = f32[128,128]{1,0:T(8,128)S(1)} collective-permute-done((f32[128,128]{1,0:T(8,128)S(1)}, f32[128,128]{1,0:T(8,128)S(1)}, u32[]{:S(2)}, u32[]{:S(2)}) %collective-permute-start.9) | collective-permute-done | bytes 65568 | tf_op jit(solution)/shard_map/ppermute | solution.py:388
  90.6 2.5 %collective-permute-start.10 = (f32[128,128]{1,0:T(8,128)S(1)}, f32[128,128]{1,0:T(8,128)S(1)}, u32[]{:S(2)}, u32[]{:S(2)}) collective-permute-start(f32[128,128]{1,0:T(8,128)S(1)} %add.38), channel_id=1, source_target_pairs={{0,64},{1,65},{2,66},{3,67},{4,68},{5,69},{6,70},{7,71},{8,72},{9,... | collective-permute-start | bytes 196616 | tf_op jit(solution)/shard_map/ppermute | solution.py:388
  93.1 1.7 %collective-permute-done.10 = f32[128,128]{1,0:T(8,128)S(1)} collective-permute-done((f32[128,128]{1,0:T(8,128)S(1)}, f32[128,128]{1,0:T(8,128)S(1)}, u32[]{:S(2)}, u32[]{:S(2)}) %collective-permute-start.10) | collective-permute-done | bytes 65568 | tf_op jit(solution)/shard_map/ppermute | solution.py:388
  94.8 5.9 %collective-permute-start.11 = (f32[128,128]{1,0:T(8,128)S(1)}, f32[128,128]{1,0:T(8,128)S(1)}, u32[]{:S(2)}, u32[]{:S(2)}) collective-permute-start(f32[128,128]{1,0:T(8,128)S(1)} %add.39), channel_id=1, source_target_pairs={{0,128},{1,129},{2,130},{3,131},{4,132},{5,133},{6,134},{7,135},{8... | collective-permute-start | bytes 196616 | tf_op jit(solution)/shard_map/ppermute | solution.py:388
  100.7 1.7 %collective-permute-done.11 = f32[128,128]{1,0:T(8,128)S(1)} collective-permute-done((f32[128,128]{1,0:T(8,128)S(1)}, f32[128,128]{1,0:T(8,128)S(1)}, u32[]{:S(2)}, u32[]{:S(2)}) %collective-permute-start.11) | collective-permute-done | bytes 65568 | tf_op jit(solution)/shard_map/ppermute | solution.py:388
  102.4 13.5 %rotation.3 = (f32[128,128]{1,0:T(8,128)S(1)}, f32[64,128]{1,0:T(8,128)}) custom-call(s32[1]{0:T(128)} %bitcast.1.flag_ref, f32[128,128]{1,0:T(8,128)S(1)} %add.40.gram_ref), custom_call_target="tpu_custom_call" | custom-call | tf_op jit(solution)/shard_map/rotation/pallas_call | solution.py:113
  115.9 8.4 %collective-permute-start.12 = (f32[128,128]{1,0:T(8,128)S(1)}, f32[128,128]{1,0:T(8,128)S(1)}, u32[]{:S(2)}, u32[]{:S(2)}) collective-permute-start(f32[128,128]{1,0:T(8,128)S(1)} %get-tuple-element.27.mine_ref), channel_id=1, source_target_pairs={{0,16},{1,17},{2,18},{3,19},{4,20},{5,21},{6,22},{7,23},{8,24},{9,... | collective-permute-start | bytes 196616 | tf_op jit(solution)/shard_map/ppermute | solution.py:388
  124.3 0.1 pad_add_fusion.flags_ref
  124.3 0.0 collective-permute-done.14.refs_7_
  124.3 0.0 collective-permute-done.13.refs_3_
  124.3 0.8 collective-permute-done.12.other_ref
  125.2 8.0 %finish.1 = f32[12288,128]{1,0:T(8,128)} custom-call(s32[2]{0:T(128)S(1)} %pad_add_fusion.flags_ref, f32[128,128]{1,0:T(8,128)S(1)} %get-tuple-element.27.mine_ref, f32[128,128]{1,0:T(8,128)S(1)} %collective-permute-done.12.other_ref, f32[3072,128]{1,0:T(8,128)S(1)} %get-tuple-element.28.refs_0_, f32[3072,128]{1,0:T(8,128)S(1)} %get-tuple-element.29.own_ref.refs_1_, ...), custom_call_target="tpu_custom_call" | custom-call | tf_op jit(solution)/shard_map/finish/pallas_call | solution.py:363
  (9 shorter events, 0.1 us)
Async XLA Ops:
  0.0 29.2 %copy-start.1 = (s32[16]{0:T(128)S(1)}, s32[16]{0:T(128)}, u32[]{:S(2)}) copy-start(s32[16]{0:T(128)} %param.3) | copy-start | bytes 196
  6.2 61.9 %collective-permute-start.5 = (f32[6144,128]{1,0:T(8,128)}, f32[6144,128]{1,0:T(8,128)S(1)}, u32[]{:S(2)}, u32[]{:S(2)}) collective-permute-start(f32[6144,128]{1,0:T(8,128)} %get-tuple-element.24.x_ref), channel_id=1, source_target_pairs={{0,1},{1,2},{2,3},{3,4},{4,5},{5,6},{6,7},{7,8},{8,9},{9,10},{10,1... | collective-permute-start | bytes 9437192 | tf_op jit(solution)/shard_map/ppermute | solution.py:388
  12.0 1.3 collective-permute-start
  13.3 4.0 %collective-permute-start.1 = (f32[128,128]{1,0:T(8,128)S(1)}, f32[128,128]{1,0:T(8,128)S(1)}, u32[]{:S(2)}, u32[]{:S(2)}) collective-permute-start(f32[128,128]{1,0:T(8,128)S(1)} %add.33), channel_id=1, source_target_pairs={{0,32},{1,33},{2,34},{3,35},{4,36},{5,37},{6,38},{7,39},{8,40},{9,... | collective-permute-start | bytes 196616 | tf_op jit(solution)/shard_map/ppermute | solution.py:388
  17.3 5.0 %collective-permute-start.2 = (f32[128,128]{1,0:T(8,128)S(1)}, f32[128,128]{1,0:T(8,128)S(1)}, u32[]{:S(2)}, u32[]{:S(2)}) collective-permute-start(f32[128,128]{1,0:T(8,128)S(1)} %add.34), channel_id=1, source_target_pairs={{0,64},{1,65},{2,66},{3,67},{4,68},{5,69},{6,70},{7,71},{8,72},{9,... | collective-permute-start | bytes 196616 | tf_op jit(solution)/shard_map/ppermute | solution.py:388
  22.4 8.5 %collective-permute-start.3 = (f32[128,128]{1,0:T(8,128)S(1)}, f32[128,128]{1,0:T(8,128)S(1)}, u32[]{:S(2)}, u32[]{:S(2)}) collective-permute-start(f32[128,128]{1,0:T(8,128)S(1)} %add.35), channel_id=1, source_target_pairs={{0,128},{1,129},{2,130},{3,131},{4,132},{5,133},{6,134},{7,135},{8... | collective-permute-start | bytes 196616 | tf_op jit(solution)/shard_map/ppermute | solution.py:388
  43.8 1.9 %copy-start = (f32[6144,128]{1,0:T(8,128)S(1)}, f32[6144,128]{1,0:T(8,128)}, u32[]{:S(2)}) copy-start(f32[6144,128]{1,0:T(8,128)} %get-tuple-element.20.x_ref) | copy-start | bytes 9437188
  48.1 20.0 %collective-permute-start.6 = (f32[3072,128]{1,0:T(8,128)S(1)}, f32[3072,128]{1,0:T(8,128)S(1)}, u32[]{:S(2)}, u32[]{:S(2)}) collective-permute-start(f32[3072,128]{1,0:T(8,128)S(1)} %get-tuple-element.21.refs_4_), channel_id=1, source_target_pairs={{0,1},{1,2},{2,3},{3,4},{4,5},{5,6},{6,7},{7,8},{8,9},{9,10},{10,1... | collective-permute-start | bytes 4718600 | tf_op jit(solution)/shard_map/ppermute | solution.py:388
  48.4 3.8 %collective-permute-start.4 = (f32[64,128]{1,0:T(8,128)S(1)}, f32[64,128]{1,0:T(8,128)S(1)}, u32[]{:S(2)}, u32[]{:S(2)}) collective-permute-start(f32[64,128]{1,0:T(8,128)S(1)} %get-tuple-element.22), channel_id=1, source_target_pairs={{0,31},{1,16},{2,17},{3,18},{4,19},{5,20},{6,21},{7,22},{8,23},{9,... | collective-permute-start | bytes 98312 | tf_op jit(solution)/shard_map/ppermute | solution.py:388
  68.1 56.2 %collective-permute-start.14 = (f32[3072,128]{1,0:T(8,128)S(1)}, f32[3072,128]{1,0:T(8,128)S(1)}, u32[]{:S(2)}, u32[]{:S(2)}) collective-permute-start(f32[3072,128]{1,0:T(8,128)S(1)} %get-tuple-element.30.own_ref.refs_5_), channel_id=1, source_target_pairs={{0,15},{1,0},{2,1},{3,2},{4,3},{5,4},{6,5},{7,6},{8,7},{9,8},{10,9... | collective-permute-start | bytes 4718600 | tf_op jit(solution)/shard_map/ppermute | solution.py:388
  68.1 56.2 %collective-permute-start.13 = (f32[3072,128]{1,0:T(8,128)S(1)}, f32[3072,128]{1,0:T(8,128)S(1)}, u32[]{:S(2)}, u32[]{:S(2)}) collective-permute-start(f32[3072,128]{1,0:T(8,128)S(1)} %get-tuple-element.29.own_ref.refs_1_), channel_id=1, source_target_pairs={{0,15},{1,0},{2,1},{3,2},{4,3},{5,4},{6,5},{7,6},{8,7},{9,8},{10,9... | collective-permute-start | bytes 4718600 | tf_op jit(solution)/shard_map/ppermute | solution.py:388
  74.7 8.2 %collective-permute-start.7 = (f32[128,128]{1,0:T(8,128)S(1)}, f32[128,128]{1,0:T(8,128)S(1)}, u32[]{:S(2)}, u32[]{:S(2)}) collective-permute-start(f32[128,128]{1,0:T(8,128)S(1)} %pair_gram.3), channel_id=1, source_target_pairs={{0,16},{1,17},{2,18},{3,19},{4,20},{5,21},{6,22},{7,23},{8,24},{9,... | collective-permute-start | bytes 196616 | tf_op jit(solution)/shard_map/ppermute | solution.py:388
  82.9 4.2 %collective-permute-start.8 = (f32[128,128]{1,0:T(8,128)S(1)}, f32[128,128]{1,0:T(8,128)S(1)}, u32[]{:S(2)}, u32[]{:S(2)}) collective-permute-start(f32[128,128]{1,0:T(8,128)S(1)} %collective-permute-done.7), channel_id=1, source_target_pairs={{0,1},{1,2},{2,3},{3,4},{4,5},{5,6},{6,7},{7,8},{8,9},{9,10},{10,1... | collective-permute-start | bytes 196616 | tf_op jit(solution)/shard_map/ppermute | solution.py:388
  87.1 3.5 %collective-permute-start.9 = (f32[128,128]{1,0:T(8,128)S(1)}, f32[128,128]{1,0:T(8,128)S(1)}, u32[]{:S(2)}, u32[]{:S(2)}) collective-permute-start(f32[128,128]{1,0:T(8,128)S(1)} %add.37), channel_id=1, source_target_pairs={{0,32},{1,33},{2,34},{3,35},{4,36},{5,37},{6,38},{7,39},{8,40},{9,... | collective-permute-start | bytes 196616 | tf_op jit(solution)/shard_map/ppermute | solution.py:388
  90.6 4.1 %collective-permute-start.10 = (f32[128,128]{1,0:T(8,128)S(1)}, f32[128,128]{1,0:T(8,128)S(1)}, u32[]{:S(2)}, u32[]{:S(2)}) collective-permute-start(f32[128,128]{1,0:T(8,128)S(1)} %add.38), channel_id=1, source_target_pairs={{0,64},{1,65},{2,66},{3,67},{4,68},{5,69},{6,70},{7,71},{8,72},{9,... | collective-permute-start | bytes 196616 | tf_op jit(solution)/shard_map/ppermute | solution.py:388
  94.8 7.6 %collective-permute-start.11 = (f32[128,128]{1,0:T(8,128)S(1)}, f32[128,128]{1,0:T(8,128)S(1)}, u32[]{:S(2)}, u32[]{:S(2)}) collective-permute-start(f32[128,128]{1,0:T(8,128)S(1)} %add.39), channel_id=1, source_target_pairs={{0,128},{1,129},{2,130},{3,131},{4,132},{5,133},{6,134},{7,135},{8... | collective-permute-start | bytes 196616 | tf_op jit(solution)/shard_map/ppermute | solution.py:388
  115.9 9.3 %collective-permute-start.12 = (f32[128,128]{1,0:T(8,128)S(1)}, f32[128,128]{1,0:T(8,128)S(1)}, u32[]{:S(2)}, u32[]{:S(2)}) collective-permute-start(f32[128,128]{1,0:T(8,128)S(1)} %get-tuple-element.27.mine_ref), channel_id=1, source_target_pairs={{0,16},{1,17},{2,18},{3,19},{4,20},{5,21},{6,22},{7,23},{8,24},{9,... | collective-permute-start | bytes 196616 | tf_op jit(solution)/shard_map/ppermute | solution.py:388

commit v3 on v2

--- a/solution.py
+++ b/solution.py
@@ -14,6 +14,7 @@
 TILE = 512
 RAW_TILES = 6
 GRAM_LIMIT = 48
+ROTATION_LIMIT = 16
 F32 = jnp.float32
 BF16 = jnp.bfloat16
 
@@ -57,41 +58,47 @@
 def orthonormal_rows(normal, rows_in):
     done = []
     spot = lax.broadcasted_iota(jnp.int32, (GROUP, ORDER), 0)
+    head_c = [across(normal[:GROUP, j : j + 1], GROUP) for j in range(GROUP)]
     for start in range(0, ORDER, GROUP):
-        tail = ORDER - start - GROUP
+        tail, after = ORDER - start - GROUP, start + GROUP
         head_n, head_y = normal[:GROUP], rows_in[:GROUP]
         tail_n, tail_y = normal[GROUP:], rows_in[GROUP:]
-        head_c = [across(head_n[:, start + j : start + j + 1], GROUP) for j in range(GROUP)]
-        tail_c = [across(tail_n[:, start + j : start + j + 1], tail) for j in range(GROUP)] if tail else []
-        pivots = head_c[0]
+        tail_c, next_c = [], []
+        if tail:
+            tail_c = [across(tail_n[:, start + j : start + j + 1], tail) for j in range(GROUP)]
+            next_c = [across(tail_n[:GROUP, after + j : after + j + 1], GROUP) for j in range(GROUP)]
+        pivots = None
         for k in range(GROUP):
             pivot = across(head_c[k][k : k + 1], GROUP)
             inverse = 1.0 / pivot
             row_n = head_n[k : k + 1]
             row_y = head_y[k : k + 1]
-            if k:
-                pivots = jnp.where(spot >= k, pivot, pivots)
-            else:
-                pivots = pivot
+            pivots = jnp.where(spot >= k, pivot, pivots) if k else pivot
             cross = [head_c[j][k : k + 1] for j in range(k + 1, GROUP)]
             if k < GROUP - 1:
                 scaled = jnp.where(spot > k, head_c[k] * inverse, 0.0)
-                head_n = head_n - scaled * row_n
-                head_y = head_y - scaled * row_y
                 for j in range(k + 1, GROUP):
                     head_c[j] = head_c[j] - scaled * cross[j - k - 1]
+                if tail:
+                    head_n = head_n - scaled * row_n
+                head_y = head_y - scaled * row_y
             if tail:
-                scaled = tail_c[k] * inverse[:1]
-                tail_n = tail_n - scaled * row_n
-                tail_y = tail_y - scaled * row_y
+                column = tail_c[k]
+                scaled = column * inverse[:1]
                 for j in range(k + 1, GROUP):
                     tail_c[j] = tail_c[j] - scaled * cross[j - k - 1]
+                for j in range(GROUP):
+                    next_c[j] = next_c[j] - scaled[:GROUP] * column[j : j + 1]
+                if tail > GROUP:
+                    tail_n = tail_n - scaled * row_n
+                tail_y = tail_y - scaled * row_y
         done.append(head_y * lax.rsqrt(pivots))
-        normal, rows_in = tail_n, tail_y
+        normal, rows_in, head_c = tail_n, tail_y, next_c
     return jnp.concatenate(done, axis=0)
 
 
-def rotation_kernel(flag_ref, gram_ref, out_ref, half_ref):
+def rotation_kernel(flag_ref, gram_ref, *refs):
+    out_ref, half_ref = refs[-2:]
     gram = gram_ref[...]
     gram = gram * (1.0 / jnp.max(jnp.abs(gram)))
 
@@ -108,7 +115,7 @@
     half_ref[...] = jnp.where(flag_ref[0] == 1, out_ref[:HALF], out_ref[HALF:])
 
 
-def rotation_rows(flag, gram_total):
+def rotation_rows(flag, gram_total, *beside):
     vmem = pl.BlockSpec(memory_space=pltpu.VMEM)
     return pl.pallas_call(
         rotation_kernel,
@@ -116,11 +123,11 @@
             jax.ShapeDtypeStruct((ORDER, ORDER), F32),
             jax.ShapeDtypeStruct((HALF, ORDER), F32),
         ),
-        in_specs=[pl.BlockSpec(memory_space=pltpu.SMEM), vmem],
+        in_specs=[pl.BlockSpec(memory_space=pltpu.SMEM), vmem] + [vmem] * len(beside),
         out_specs=(vmem, vmem),
-        compiler_params=limit(8),
+        compiler_params=limit(ROTATION_LIMIT),
         name="rotation",
-    )(flag, gram_total)
+    )(flag, gram_total, *beside)
 
 
 def vmem():
@@ -137,6 +144,10 @@
 
 def tile_rows(tile, size):
     return pl.ds(pl.multiple_of(tile * size, size), size)
+
+
+def cost(flops, moved_bytes):
+    return pl.CostEstimate(flops=flops, bytes_accessed=moved_bytes, transcendentals=0)
 
 
 def gram_kernel(x_ref, out_ref, sent_ref, rest_ref, held, sems, sent_sems):
@@ -183,6 +194,7 @@
             pltpu.SemaphoreType.DMA((RAW_TILES,)),
         ],
         compiler_params=limit(GRAM_LIMIT),
+        cost_estimate=cost(4 * rows * ORDER * ORDER, 4 * rows * ORDER),
         name="gram",
     )(columns)
 
@@ -216,7 +228,7 @@
     lower = jnp.concatenate([none, early, none, late], axis=0)
     store_weights(jnp.concatenate([upper, lower], axis=1).T, high, low)
 
-    @pl.loop(0, early_ref.shape[0] // TILE)
+    @pl.loop(0, early_ref.shape[0] // TILE, unroll=True)
     def _(tile):
         out = dot_three(packed(x_ref, tile), high, low)
         early_ref[tile_rows(tile, TILE)] = out[:, :ORDER]
@@ -232,6 +244,7 @@
         out_specs=(vmem(), vmem()),
         scratch_shapes=[pltpu.VMEM((2 * ORDER, 2 * ORDER), BF16)] * 2,
         compiler_params=limit(16),
+        cost_estimate=cost(12 * columns.shape[0] * ORDER * ORDER, 8 * columns.shape[0] * ORDER),
         name="turn",
     )(early_is_back, turn_rows, columns)
 
@@ -243,7 +256,7 @@
     lower = jnp.concatenate([none, rows], axis=0)
     store_weights(jnp.concatenate([upper, lower], axis=1).T, high, low)
 
-    @pl.loop(0, out_ref.shape[0] // TILE)
+    @pl.loop(0, out_ref.shape[0] // TILE, unroll=True)
     def _(tile):
         out_ref[tile_rows(tile, TILE)] = dot_three(packed(x_ref, tile), high, low)
 
@@ -256,6 +269,7 @@
         out_specs=vmem(),
         scratch_shapes=[pltpu.VMEM((2 * ORDER, ORDER), BF16)] * 2,
         compiler_params=limit(16),
+        cost_estimate=cost(8 * columns.shape[0] * ORDER * ORDER, 6 * columns.shape[0] * ORDER),
         name="turn_raw",
     )(half_rows, columns)
 
@@ -271,7 +285,7 @@
 def pair_gram_kernel(core_ref, before_ref, own_ref, come_ref, out_ref, total):
     total[...] = jnp.zeros_like(total)
 
-    @pl.loop(0, own_ref.shape[0] // TILE)
+    @pl.loop(0, own_ref.shape[0] // TILE, unroll=True)
     def _(tile):
         rows = tile_rows(tile, TILE)
         high, low = split_two(jnp.concatenate([own_ref[rows], come_ref[rows]], axis=1))
@@ -297,6 +311,7 @@
         out_specs=vmem(),
         scratch_shapes=[pltpu.VMEM((2 * ORDER, 4 * ORDER), F32)],
         compiler_params=limit(16),
+        cost_estimate=cost(16 * own.shape[0] * ORDER * ORDER, 8 * own.shape[0] * ORDER),
         name="pair_gram",
     )(core, before, own, come)
 
@@ -343,7 +358,7 @@
     for index, (place, tiles) in enumerate(places):
         early_ref, late_ref, come_ref, last_ref = parts[4 * index : 4 * index + 4]
 
-        @pl.loop(0, tiles)
+        @pl.loop(0, tiles, unroll=True)
         def _(tile):
             rows = tile_rows(tile, TILE)
             early = jnp.concatenate([early_ref[rows], last_ref[rows]], axis=1)
@@ -428,7 +443,7 @@
     gram, sent, rest = gram_and_rows(matrix)
     raw_come = moved(sent, outward)
     gram = gram + moved(gram, swap_rows(1))
-    first_turn, half_turn = rotation_rows(flag, summed(gram))
+    first_turn, half_turn = rotation_rows(flag, summed(gram), rest)
     come_turn = moved(half_turn, inward_swapped)
 
     early_b, late_b = turn(rest, first_turn, flag)
@@ -437,8 +452,8 @@
     come_a = turn_raw(raw_come, come_turn)
     second = pair_gram(core_flag, jnp.zeros_like(gram), late_a, come_a)
     second = pair_gram(core_flag, second, late_b, come_b)
-    last_a = moved(tied(late_a, come_b), inward)
-    last_b = moved(tied(late_b, come_b, come_turn), inward)
+    last_a = moved(tied(late_a, second), inward)
+    last_b = moved(tied(late_b, second), inward)
     second = second + moved(moved(second, swap_rows(1)), outward)
     mine, _ = rotation_rows(flag, summed(second))
     other = moved(mine, swap_rows(1))

time: 134 us -> 121 us (0.903)
  Pallas kernels: 53.9 us -> 41.8 us
    pallas_call x2, Pallas kernels: 26.4 us -> 21.9 us  [rotation_rows(): pl.pallas_call(rotation_kernel, out_shape=(jax.ShapeDtypeStruct((ORDER, O...]
    pallas_call x1, Pallas kernels: 8.02 us -> 5.33 us  [finish(): pl.pallas_call(functools.partial(finish_kernel, places), out_shape=jax.Sh...]
    pallas_call x2, Pallas kernels: 4.53 us -> 2.44 us  [pair_gram(): pl.pallas_call(pair_gram_kernel, out_shape=jax.ShapeDtypeStruct((ORDER, O...]
    pallas_call x2, Pallas kernels: 6.68 us -> 4.91 us  [turn(): pl.pallas_call(turn_kernel, out_shape=(half, half), in_specs=[smem(), vme...]
  transfers between devices with their start and end apart: 15 -> 15, of which waited for: 12 -> 12; matrix products, arithmetic and copies ran while one was open for 1% -> 1% of each run, Pallas kernels for 30% -> 24%
where the time goes in v3:
time: 121 us
  starting transfers between devices  44.9 us (37%)
  Pallas kernels  41.8 us (35%)
  waiting for transfers between devices  30.5 us (25%)
  local copies, waits for them, and re-layouts  2.47 us (2%)
    ppermute x15, starting transfers between devices, moved(): return lax.ppermute(array, ('row', 'col'), pairs)  44.9 us
    ppermute x15, waiting for transfers between devices, moved(): return lax.ppermute(array, ('row', 'col'), pairs)  30.5 us
    pallas_call x2, Pallas kernels, rotation_rows(): pl.pallas_call(rotation_kernel, out_shape=(jax.ShapeDtypeStruct((ORDER, O...  21.9 us
    pallas_call x1, Pallas kernels, gram_and_rows(): pl.pallas_call(gram_kernel, out_shape=(jax.ShapeDtypeStruct((ORDER, ORDER...  6.18 us
    pallas_call x1, Pallas kernels, finish(): pl.pallas_call(functools.partial(finish_kernel, places), out_shape=jax.Sh...  5.33 us
    pallas_call x2, Pallas kernels, turn(): pl.pallas_call(turn_kernel, out_shape=(half, half), in_specs=[smem(), vme...  4.91 us
    pallas_call x2, Pallas kernels, pair_gram(): pl.pallas_call(pair_gram_kernel, out_shape=jax.ShapeDtypeStruct((ORDER, O...  2.44 us
  transfers between devices with their start and end apart: 15, of which 12 were waited for; matrix products, arithmetic and copies ran while one was open for 1% of the time, Pallas kernels for 24%

profile of v3, /device:TPU:1, one launch (start us, length us, event | category | flops | bytes accessed | tf_op | source)
XLA Modules:
  0.0 120.8 jit_solution(9033688375817312208)
XLA Ops:
  0.0 0.0 copy-start.1
  0.0 6.2 %gram.1 = (f32[128,128]{1,0:T(8,128)S(1)}, f32[6144,128]{1,0:T(8,128)}, f32[6144,128]{1,0:T(8,128)}) custom-call(f32[12288,128]{1,0:T(8,128)} %x_ref.1), custom_call_target="tpu_custom_call" | custom-call | flops 805306368 | bytes 6291456 | tf_op jit(solution)/shard_map/gram/pallas_call | solution.py:182
  6.2 5.8 %collective-permute-start.5 = (f32[6144,128]{1,0:T(8,128)}, f32[6144,128]{1,0:T(8,128)S(1)}, u32[]{:S(2)}, u32[]{:S(2)}) collective-permute-start(f32[6144,128]{1,0:T(8,128)} %get-tuple-element.24.x_ref), channel_id=1, source_target_pairs={{0,1},{1,2},{2,3},{3,4},{4,5},{5,6},{6,7},{7,8},{8,9},{9,10},{10,1... | collective-permute-start | bytes 9437192 | tf_op jit(solution)/shard_map/ppermute | solution.py:403
  12.0 0.0 collective-permute-start
  12.0 1.3 %collective-permute-done = f32[128,128]{1,0:T(8,128)S(1)} collective-permute-done((f32[128,128]{1,0:T(8,128)S(1)}, f32[128,128]{1,0:T(8,128)S(1)}, u32[]{:S(2)}, u32[]{:S(2)}) %collective-permute-start) | collective-permute-done | bytes 65568 | tf_op jit(solution)/shard_map/ppermute | solution.py:403
  13.3 1.7 %collective-permute-start.1 = (f32[128,128]{1,0:T(8,128)S(1)}, f32[128,128]{1,0:T(8,128)S(1)}, u32[]{:S(2)}, u32[]{:S(2)}) collective-permute-start(f32[128,128]{1,0:T(8,128)S(1)} %add.33), channel_id=1, source_target_pairs={{0,32},{1,33},{2,34},{3,35},{4,36},{5,37},{6,38},{7,39},{8,40},{9,... | collective-permute-start | bytes 196616 | tf_op jit(solution)/shard_map/ppermute | solution.py:403
  15.0 2.3 %collective-permute-done.1 = f32[128,128]{1,0:T(8,128)S(1)} collective-permute-done((f32[128,128]{1,0:T(8,128)S(1)}, f32[128,128]{1,0:T(8,128)S(1)}, u32[]{:S(2)}, u32[]{:S(2)}) %collective-permute-start.1) | collective-permute-done | bytes 65568 | tf_op jit(solution)/shard_map/ppermute | solution.py:403
  17.3 3.1 %collective-permute-start.2 = (f32[128,128]{1,0:T(8,128)S(1)}, f32[128,128]{1,0:T(8,128)S(1)}, u32[]{:S(2)}, u32[]{:S(2)}) collective-permute-start(f32[128,128]{1,0:T(8,128)S(1)} %add.34), channel_id=1, source_target_pairs={{0,64},{1,65},{2,66},{3,67},{4,68},{5,69},{6,70},{7,71},{8,72},{9,... | collective-permute-start | bytes 196616 | tf_op jit(solution)/shard_map/ppermute | solution.py:403
  20.4 2.0 %collective-permute-done.2 = f32[128,128]{1,0:T(8,128)S(1)} collective-permute-done((f32[128,128]{1,0:T(8,128)S(1)}, f32[128,128]{1,0:T(8,128)S(1)}, u32[]{:S(2)}, u32[]{:S(2)}) %collective-permute-start.2) | collective-permute-done | bytes 65568 | tf_op jit(solution)/shard_map/ppermute | solution.py:403
  22.4 6.9 %collective-permute-start.3 = (f32[128,128]{1,0:T(8,128)S(1)}, f32[128,128]{1,0:T(8,128)S(1)}, u32[]{:S(2)}, u32[]{:S(2)}) collective-permute-start(f32[128,128]{1,0:T(8,128)S(1)} %add.35), channel_id=1, source_target_pairs={{0,128},{1,129},{2,130},{3,131},{4,132},{5,133},{6,134},{7,135},{8... | collective-permute-start | bytes 196616 | tf_op jit(solution)/shard_map/ppermute | solution.py:403
  29.2 0.0 copy-done.1
  29.2 0.6 dynamic_slice.3
  30.4 0.5 collective-permute-done.3
  30.9 0.0 copy-start
  30.9 1.9 %copy-done = f32[6144,128]{1,0:T(8,128)S(1)} copy-done((f32[6144,128]{1,0:T(8,128)S(1)}, f32[6144,128]{1,0:T(8,128)}, u32[]{:S(2)}) %copy-start) | copy-done | bytes 3145752
  32.8 10.6 %rotation.2 = (f32[128,128]{1,0:T(8,128)S(1)}, f32[64,128]{1,0:T(8,128)S(1)}) custom-call(s32[1]{0:T(128)} %bitcast.1.flag_ref, f32[128,128]{1,0:T(8,128)S(1)} %add.36.gram_ref, f32[6144,128]{1,0:T(8,128)S(1)} %copy-done), custom_call_target="tpu_custom_call" | custom-call | tf_op jit(solution)/shard_map/rotation/pallas_call | solution.py:120
  43.4 1.5 %turn.2 = (f32[3072,128]{1,0:T(8,128)S(1)}, f32[3072,128]{1,0:T(8,128)S(1)}) custom-call(s32[1]{0:T(128)} %bitcast.1.flag_ref, f32[128,128]{1,0:T(8,128)S(1)} %get-tuple-element.23.rows_ref, f32[6144,128]{1,0:T(8,128)S(1)} %copy-done), custom_call_target="tpu_custom_call" | custom-call | flops 1207959552 | bytes 6291456 | tf_op jit(solution)/shard_map/turn/pallas_call | solution.py:240
  45.0 0.3 collective-permute-start.6
  45.2 1.9 %collective-permute-start.4 = (f32[64,128]{1,0:T(8,128)S(1)}, f32[64,128]{1,0:T(8,128)S(1)}, u32[]{:S(2)}, u32[]{:S(2)}) collective-permute-start(f32[64,128]{1,0:T(8,128)S(1)} %get-tuple-element.22), channel_id=1, source_target_pairs={{0,31},{1,16},{2,17},{3,18},{4,19},{5,20},{6,21},{7,22},{8,23},{9,... | collective-permute-start | bytes 98312 | tf_op jit(solution)/shard_map/ppermute | solution.py:403
  47.1 2.2 %collective-permute-done.4.rows_ref = f32[64,128]{1,0:T(8,128)S(1)} collective-permute-done((f32[64,128]{1,0:T(8,128)S(1)}, f32[64,128]{1,0:T(8,128)S(1)}, u32[]{:S(2)}, u32[]{:S(2)}) %collective-permute-start.4) | collective-permute-done | bytes 32800 | tf_op jit(solution)/shard_map/ppermute | solution.py:403
  49.3 3.4 %turn.3 = (f32[3072,128]{1,0:T(8,128)S(1)}, f32[3072,128]{1,0:T(8,128)S(1)}) custom-call(s32[1]{0:T(128)} %bitcast.1.flag_ref, f32[128,128]{1,0:T(8,128)S(1)} %get-tuple-element.23.rows_ref, f32[6144,128]{1,0:T(8,128)} %get-tuple-element.24.x_ref), custom_call_target="tpu_custom_call" | custom-call | flops 1207959552 | bytes 6291456 | tf_op jit(solution)/shard_map/turn/pallas_call | solution.py:240
  52.7 0.0 collective-permute-done.5.x_ref
  52.7 1.1 turn_raw.1.come_ref.refs_2_
  53.8 1.2 %pair_gram.2.before_ref = f32[128,128]{1,0:T(8,128)S(1)} custom-call(s32[1]{0:T(128)} %bitcast.2.core_ref, f32[128,128]{1,0:T(8,128)S(1)} %broadcast_in_dim.3.before_ref, f32[3072,128]{1,0:T(8,128)S(1)} %get-tuple-element.29.own_ref.refs_1_, f32[3072,128]{1,0:T(8,128)S(1)} %turn_raw.1.come_ref.refs_2_), custom_call_target="tpu_custom_call" | custom-call | flops 805306368 | bytes 3145728 | tf_op jit(solution)/shard_map/pair_gram/pallas_call | solution.py:307
  55.1 9.9 %collective-permute-done.6.come_ref.refs_6_ = f32[3072,128]{1,0:T(8,128)S(1)} collective-permute-done((f32[3072,128]{1,0:T(8,128)S(1)}, f32[3072,128]{1,0:T(8,128)S(1)}, u32[]{:S(2)}, u32[]{:S(2)}) %collective-permute-start.6) | collective-permute-done | bytes 1572896 | tf_op jit(solution)/shard_map/ppermute | solution.py:403
  64.9 1.2 %pair_gram.3 = f32[128,128]{1,0:T(8,128)S(1)} custom-call(s32[1]{0:T(128)} %bitcast.2.core_ref, f32[128,128]{1,0:T(8,128)S(1)} %pair_gram.2.before_ref, f32[3072,128]{1,0:T(8,128)S(1)} %get-tuple-element.30.own_ref.refs_5_, f32[3072,128]{1,0:T(8,128)S(1)} %collective-permute-done.6.come_ref.refs_6_), custom_call_target="tpu_custom_call" | custom-call | flops 805306368 | bytes 3145728 | tf_op jit(solution)/shard_map/pair_gram/pallas_call | solution.py:307
  66.2 0.1 collective-permute-start.13
  66.3 0.1 collective-permute-start.14
  66.3 6.7 %collective-permute-start.7 = (f32[128,128]{1,0:T(8,128)S(1)}, f32[128,128]{1,0:T(8,128)S(1)}, u32[]{:S(2)}, u32[]{:S(2)}) collective-permute-start(f32[128,128]{1,0:T(8,128)S(1)} %pair_gram.3), channel_id=1, source_target_pairs={{0,16},{1,17},{2,18},{3,19},{4,20},{5,21},{6,22},{7,23},{8,24},{9,... | collective-permute-start | bytes 196616 | tf_op jit(solution)/shard_map/ppermute | solution.py:403
  73.0 0.9 collective-permute-done.7
  73.9 0.1 collective-permute-start.8
  74.1 4.1 %collective-permute-done.8 = f32[128,128]{1,0:T(8,128)S(1)} collective-permute-done((f32[128,128]{1,0:T(8,128)S(1)}, f32[128,128]{1,0:T(8,128)S(1)}, u32[]{:S(2)}, u32[]{:S(2)}) %collective-permute-start.8) | collective-permute-done | bytes 65568 | tf_op jit(solution)/shard_map/ppermute | solution.py:403
  78.2 0.4 collective-permute-start.9
  78.6 3.1 %collective-permute-done.9 = f32[128,128]{1,0:T(8,128)S(1)} collective-permute-done((f32[128,128]{1,0:T(8,128)S(1)}, f32[128,128]{1,0:T(8,128)S(1)}, u32[]{:S(2)}, u32[]{:S(2)}) %collective-permute-start.9) | collective-permute-done | bytes 65568 | tf_op jit(solution)/shard_map/ppermute | solution.py:403
  81.7 2.6 %collective-permute-start.10 = (f32[128,128]{1,0:T(8,128)S(1)}, f32[128,128]{1,0:T(8,128)S(1)}, u32[]{:S(2)}, u32[]{:S(2)}) collective-permute-start(f32[128,128]{1,0:T(8,128)S(1)} %add.38), channel_id=1, source_target_pairs={{0,64},{1,65},{2,66},{3,67},{4,68},{5,69},{6,70},{7,71},{8,72},{9,... | collective-permute-start | bytes 196616 | tf_op jit(solution)/shard_map/ppermute | solution.py:403
  84.3 1.7 %collective-permute-done.10 = f32[128,128]{1,0:T(8,128)S(1)} collective-permute-done((f32[128,128]{1,0:T(8,128)S(1)}, f32[128,128]{1,0:T(8,128)S(1)}, u32[]{:S(2)}, u32[]{:S(2)}) %collective-permute-start.10) | collective-permute-done | bytes 65568 | tf_op jit(solution)/shard_map/ppermute | solution.py:403
  86.0 6.6 %collective-permute-start.11 = (f32[128,128]{1,0:T(8,128)S(1)}, f32[128,128]{1,0:T(8,128)S(1)}, u32[]{:S(2)}, u32[]{:S(2)}) collective-permute-start(f32[128,128]{1,0:T(8,128)S(1)} %add.39), channel_id=1, source_target_pairs={{0,128},{1,129},{2,130},{3,131},{4,132},{5,133},{6,134},{7,135},{8... | collective-permute-start | bytes 196616 | tf_op jit(solution)/shard_map/ppermute | solution.py:403
  92.6 1.7 %collective-permute-done.11 = f32[128,128]{1,0:T(8,128)S(1)} collective-permute-done((f32[128,128]{1,0:T(8,128)S(1)}, f32[128,128]{1,0:T(8,128)S(1)}, u32[]{:S(2)}, u32[]{:S(2)}) %collective-permute-start.11) | collective-permute-done | bytes 65568 | tf_op jit(solution)/shard_map/ppermute | solution.py:403
  94.4 11.3 %rotation.3 = (f32[128,128]{1,0:T(8,128)S(1)}, f32[64,128]{1,0:T(8,128)}) custom-call(s32[1]{0:T(128)} %bitcast.1.flag_ref, f32[128,128]{1,0:T(8,128)S(1)} %add.40.gram_ref), custom_call_target="tpu_custom_call" | custom-call | tf_op jit(solution)/shard_map/rotation/pallas_call | solution.py:120
  105.7 8.7 %collective-permute-start.12 = (f32[128,128]{1,0:T(8,128)S(1)}, f32[128,128]{1,0:T(8,128)S(1)}, u32[]{:S(2)}, u32[]{:S(2)}) collective-permute-start(f32[128,128]{1,0:T(8,128)S(1)} %get-tuple-element.27.mine_ref), channel_id=1, source_target_pairs={{0,16},{1,17},{2,18},{3,19},{4,20},{5,21},{6,22},{7,23},{8,24},{9,... | collective-permute-start | bytes 196616 | tf_op jit(solution)/shard_map/ppermute | solution.py:403
  114.3 0.1 pad_add_fusion.flags_ref
  114.4 0.8 collective-permute-done.12.other_ref
  115.2 0.0 collective-permute-done.13.refs_3_
  115.2 0.0 collective-permute-done.14.refs_7_
  115.2 5.3 %finish.1 = f32[12288,128]{1,0:T(8,128)} custom-call(s32[2]{0:T(128)S(1)} %pad_add_fusion.flags_ref, f32[128,128]{1,0:T(8,128)S(1)} %get-tuple-element.27.mine_ref, f32[128,128]{1,0:T(8,128)S(1)} %collective-permute-done.12.other_ref, f32[3072,128]{1,0:T(8,128)S(1)} %get-tuple-element.28.refs_0_, f32[3072,128]{1,0:T(8,128)S(1)} %get-tuple-element.29.own_ref.refs_1_, ...), custom_call_target="tpu_custom_call" | custom-call | tf_op jit(solution)/shard_map/finish/pallas_call | solution.py:378
  (9 shorter events, 0.1 us)
Async XLA Ops:
  0.0 29.2 %copy-start.1 = (s32[16]{0:T(128)S(1)}, s32[16]{0:T(128)}, u32[]{:S(2)}) copy-start(s32[16]{0:T(128)} %param.3) | copy-start | bytes 196
  6.2 46.5 %collective-permute-start.5 = (f32[6144,128]{1,0:T(8,128)}, f32[6144,128]{1,0:T(8,128)S(1)}, u32[]{:S(2)}, u32[]{:S(2)}) collective-permute-start(f32[6144,128]{1,0:T(8,128)} %get-tuple-element.24.x_ref), channel_id=1, source_target_pairs={{0,1},{1,2},{2,3},{3,4},{4,5},{5,6},{6,7},{7,8},{8,9},{9,10},{10,1... | collective-permute-start | bytes 9437192 | tf_op jit(solution)/shard_map/ppermute | solution.py:403
  12.0 1.3 %collective-permute-start = (f32[128,128]{1,0:T(8,128)S(1)}, f32[128,128]{1,0:T(8,128)S(1)}, u32[]{:S(2)}, u32[]{:S(2)}) collective-permute-start(f32[128,128]{1,0:T(8,128)S(1)} %get-tuple-element.18), channel_id=1, source_target_pairs={{0,16},{1,17},{2,18},{3,19},{4,20},{5,21},{6,22},{7,23},{8,24},{9,... | collective-permute-start | bytes 196616 | tf_op jit(solution)/shard_map/ppermute | solution.py:403
  13.3 4.0 %collective-permute-start.1 = (f32[128,128]{1,0:T(8,128)S(1)}, f32[128,128]{1,0:T(8,128)S(1)}, u32[]{:S(2)}, u32[]{:S(2)}) collective-permute-start(f32[128,128]{1,0:T(8,128)S(1)} %add.33), channel_id=1, source_target_pairs={{0,32},{1,33},{2,34},{3,35},{4,36},{5,37},{6,38},{7,39},{8,40},{9,... | collective-permute-start | bytes 196616 | tf_op jit(solution)/shard_map/ppermute | solution.py:403
  17.3 5.0 %collective-permute-start.2 = (f32[128,128]{1,0:T(8,128)S(1)}, f32[128,128]{1,0:T(8,128)S(1)}, u32[]{:S(2)}, u32[]{:S(2)}) collective-permute-start(f32[128,128]{1,0:T(8,128)S(1)} %add.34), channel_id=1, source_target_pairs={{0,64},{1,65},{2,66},{3,67},{4,68},{5,69},{6,70},{7,71},{8,72},{9,... | collective-permute-start | bytes 196616 | tf_op jit(solution)/shard_map/ppermute | solution.py:403
  22.4 8.5 %collective-permute-start.3 = (f32[128,128]{1,0:T(8,128)S(1)}, f32[128,128]{1,0:T(8,128)S(1)}, u32[]{:S(2)}, u32[]{:S(2)}) collective-permute-start(f32[128,128]{1,0:T(8,128)S(1)} %add.35), channel_id=1, source_target_pairs={{0,128},{1,129},{2,130},{3,131},{4,132},{5,133},{6,134},{7,135},{8... | collective-permute-start | bytes 196616 | tf_op jit(solution)/shard_map/ppermute | solution.py:403
  30.9 1.9 %copy-start = (f32[6144,128]{1,0:T(8,128)S(1)}, f32[6144,128]{1,0:T(8,128)}, u32[]{:S(2)}) copy-start(f32[6144,128]{1,0:T(8,128)} %get-tuple-element.19.refs_0_.x_ref) | copy-start | bytes 9437188
  45.0 20.0 %collective-permute-start.6 = (f32[3072,128]{1,0:T(8,128)S(1)}, f32[3072,128]{1,0:T(8,128)S(1)}, u32[]{:S(2)}, u32[]{:S(2)}) collective-permute-start(f32[3072,128]{1,0:T(8,128)S(1)} %get-tuple-element.21.refs_4_), channel_id=1, source_target_pairs={{0,1},{1,2},{2,3},{3,4},{4,5},{5,6},{6,7},{7,8},{8,9},{9,10},{10,1... | collective-permute-start | bytes 4718600 | tf_op jit(solution)/shard_map/ppermute | solution.py:403
  45.2 4.1 %collective-permute-start.4 = (f32[64,128]{1,0:T(8,128)S(1)}, f32[64,128]{1,0:T(8,128)S(1)}, u32[]{:S(2)}, u32[]{:S(2)}) collective-permute-start(f32[64,128]{1,0:T(8,128)S(1)} %get-tuple-element.22), channel_id=1, source_target_pairs={{0,31},{1,16},{2,17},{3,18},{4,19},{5,20},{6,21},{7,22},{8,23},{9,... | collective-permute-start | bytes 98312 | tf_op jit(solution)/shard_map/ppermute | solution.py:403
  66.2 49.1 %collective-permute-start.13 = (f32[3072,128]{1,0:T(8,128)S(1)}, f32[3072,128]{1,0:T(8,128)S(1)}, u32[]{:S(2)}, u32[]{:S(2)}) collective-permute-start(f32[3072,128]{1,0:T(8,128)S(1)} %get-tuple-element.29.own_ref.refs_1_), channel_id=1, source_target_pairs={{0,15},{1,0},{2,1},{3,2},{4,3},{5,4},{6,5},{7,6},{8,7},{9,8},{10,9... | collective-permute-start | bytes 4718600 | tf_op jit(solution)/shard_map/ppermute | solution.py:403
  66.3 49.0 %collective-permute-start.14 = (f32[3072,128]{1,0:T(8,128)S(1)}, f32[3072,128]{1,0:T(8,128)S(1)}, u32[]{:S(2)}, u32[]{:S(2)}) collective-permute-start(f32[3072,128]{1,0:T(8,128)S(1)} %get-tuple-element.30.own_ref.refs_5_), channel_id=1, source_target_pairs={{0,15},{1,0},{2,1},{3,2},{4,3},{5,4},{6,5},{7,6},{8,7},{9,8},{10,9... | collective-permute-start | bytes 4718600 | tf_op jit(solution)/shard_map/ppermute | solution.py:403
  66.3 7.6 %collective-permute-start.7 = (f32[128,128]{1,0:T(8,128)S(1)}, f32[128,128]{1,0:T(8,128)S(1)}, u32[]{:S(2)}, u32[]{:S(2)}) collective-permute-start(f32[128,128]{1,0:T(8,128)S(1)} %pair_gram.3), channel_id=1, source_target_pairs={{0,16},{1,17},{2,18},{3,19},{4,20},{5,21},{6,22},{7,23},{8,24},{9,... | collective-permute-start | bytes 196616 | tf_op jit(solution)/shard_map/ppermute | solution.py:403
  73.9 4.3 %collective-permute-start.8 = (f32[128,128]{1,0:T(8,128)S(1)}, f32[128,128]{1,0:T(8,128)S(1)}, u32[]{:S(2)}, u32[]{:S(2)}) collective-permute-start(f32[128,128]{1,0:T(8,128)S(1)} %collective-permute-done.7), channel_id=1, source_target_pairs={{0,1},{1,2},{2,3},{3,4},{4,5},{5,6},{6,7},{7,8},{8,9},{9,10},{10,1... | collective-permute-start | bytes 196616 | tf_op jit(solution)/shard_map/ppermute | solution.py:403
  78.2 3.5 %collective-permute-start.9 = (f32[128,128]{1,0:T(8,128)S(1)}, f32[128,128]{1,0:T(8,128)S(1)}, u32[]{:S(2)}, u32[]{:S(2)}) collective-permute-start(f32[128,128]{1,0:T(8,128)S(1)} %add.37), channel_id=1, source_target_pairs={{0,32},{1,33},{2,34},{3,35},{4,36},{5,37},{6,38},{7,39},{8,40},{9,... | collective-permute-start | bytes 196616 | tf_op jit(solution)/shard_map/ppermute | solution.py:403
  81.7 4.3 %collective-permute-start.10 = (f32[128,128]{1,0:T(8,128)S(1)}, f32[128,128]{1,0:T(8,128)S(1)}, u32[]{:S(2)}, u32[]{:S(2)}) collective-permute-start(f32[128,128]{1,0:T(8,128)S(1)} %add.38), channel_id=1, source_target_pairs={{0,64},{1,65},{2,66},{3,67},{4,68},{5,69},{6,70},{7,71},{8,72},{9,... | collective-permute-start | bytes 196616 | tf_op jit(solution)/shard_map/ppermute | solution.py:403
  86.0 8.4 %collective-permute-start.11 = (f32[128,128]{1,0:T(8,128)S(1)}, f32[128,128]{1,0:T(8,128)S(1)}, u32[]{:S(2)}, u32[]{:S(2)}) collective-permute-start(f32[128,128]{1,0:T(8,128)S(1)} %add.39), channel_id=1, source_target_pairs={{0,128},{1,129},{2,130},{3,131},{4,132},{5,133},{6,134},{7,135},{8... | collective-permute-start | bytes 196616 | tf_op jit(solution)/shard_map/ppermute | solution.py:403
  105.7 9.6 %collective-permute-start.12 = (f32[128,128]{1,0:T(8,128)S(1)}, f32[128,128]{1,0:T(8,128)S(1)}, u32[]{:S(2)}, u32[]{:S(2)}) collective-permute-start(f32[128,128]{1,0:T(8,128)S(1)} %get-tuple-element.27.mine_ref), channel_id=1, source_target_pairs={{0,16},{1,17},{2,18},{3,19},{4,20},{5,21},{6,22},{7,23},{8,24},{9,... | collective-permute-start | bytes 196616 | tf_op jit(solution)/shard_map/ppermute | solution.py:403

commit v4 on v3

--- a/solution.py
+++ b/solution.py
@@ -14,7 +14,7 @@
 TILE = 512
 RAW_TILES = 6
 GRAM_LIMIT = 48
-ROTATION_LIMIT = 16
+ROTATION_LIMIT = 48
 F32 = jnp.float32
 BF16 = jnp.bfloat16
 
@@ -97,37 +97,34 @@
     return jnp.concatenate(done, axis=0)
 
 
-def rotation_kernel(flag_ref, gram_ref, *refs):
-    out_ref, half_ref = refs[-2:]
-    gram = gram_ref[...]
+def rotate(gram, out_ref):
     gram = gram * (1.0 / jnp.max(jnp.abs(gram)))
 
-    def turn(rows):
+    def turn_rows(rows):
         out_ref[...] = orthonormal_rows(dot_six(rows, rows, True), rows)
 
-    turn(gram)
+    turn_rows(gram)
 
     def step(_, carry):
-        turn(dot_six(out_ref[...], gram, False))
+        turn_rows(dot_six(out_ref[...], gram, False))
         return carry
 
     lax.fori_loop(1, ITERS, step, 0)
-    half_ref[...] = jnp.where(flag_ref[0] == 1, out_ref[:HALF], out_ref[HALF:])
-
-
-def rotation_rows(flag, gram_total, *beside):
-    vmem = pl.BlockSpec(memory_space=pltpu.VMEM)
+
+
+def rotation_kernel(gram_ref, out_ref):
+    rotate(gram_ref[...], out_ref)
+
+
+def rotation_rows(gram_total):
     return pl.pallas_call(
         rotation_kernel,
-        out_shape=(
-            jax.ShapeDtypeStruct((ORDER, ORDER), F32),
-            jax.ShapeDtypeStruct((HALF, ORDER), F32),
-        ),
-        in_specs=[pl.BlockSpec(memory_space=pltpu.SMEM), vmem] + [vmem] * len(beside),
-        out_specs=(vmem, vmem),
-        compiler_params=limit(ROTATION_LIMIT),
+        out_shape=jax.ShapeDtypeStruct((ORDER, ORDER), F32),
+        in_specs=[vmem()],
+        out_specs=vmem(),
+        compiler_params=limit(16),
         name="rotation",
-    )(flag, gram_total, *beside)
+    )(gram_total)
 
 
 def vmem():
@@ -150,16 +147,14 @@
     return pl.CostEstimate(flops=flops, bytes_accessed=moved_bytes, transcendentals=0)
 
 
-def gram_kernel(x_ref, out_ref, sent_ref, rest_ref, held, sems, sent_sems):
+def gram_kernel(x_ref, out_ref, sent_ref, held, sems, sent_sems):
     size = 2 * TILE
-    places, copies, sends = [], [], []
-    for tile in range(x_ref.shape[0] // size):
+    copies, sends = [], []
+    for tile in range(held.shape[0]):
         rows = pl.ds(tile * size, size)
-        place = held.at[rows] if tile < RAW_TILES else rest_ref.at[pl.ds((tile - RAW_TILES) * size, size)]
-        places.append(place)
-        copies.append(pltpu.make_async_copy(x_ref.at[rows], place, sems.at[tile]))
+        copies.append(pltpu.make_async_copy(x_ref.at[rows], held.at[tile], sems.at[tile]))
         if tile < RAW_TILES:
-            sends.append(pltpu.make_async_copy(place, sent_ref.at[rows], sent_sems.at[tile]))
+            sends.append(pltpu.make_async_copy(held.at[tile], sent_ref.at[rows], sent_sems.at[tile]))
     for copy in copies:
         copy.start()
     total = jnp.zeros((ORDER, 2 * ORDER), F32)
@@ -167,7 +162,7 @@
         copy.wait()
         if tile < RAW_TILES:
             sends[tile].start()
-        high, low = split_two(places[tile][...])
+        high, low = split_two(held[tile])
         total = total + dot_bf16(high, jnp.concatenate([high, low], axis=1), ((0,), (0,)))
     mixed = total[:, ORDER:]
     out_ref[...] = total[:, :ORDER] + (mixed + mixed.T)
@@ -175,21 +170,19 @@
         send.wait()
 
 
-def gram_and_rows(columns):
+def gram_and_raw(columns):
     rows = columns.shape[0]
     tiles = rows // (2 * TILE)
-    raw_rows = RAW_TILES * 2 * TILE
     return pl.pallas_call(
         gram_kernel,
         out_shape=(
             jax.ShapeDtypeStruct((ORDER, ORDER), F32),
-            jax.ShapeDtypeStruct((raw_rows, ORDER), F32),
-            jax.ShapeDtypeStruct((rows - raw_rows, ORDER), F32),
+            jax.ShapeDtypeStruct((RAW_TILES * 2 * TILE, ORDER), F32),
         ),
         in_specs=[pl.BlockSpec(memory_space=pl.ANY)],
-        out_specs=(vmem(), pl.BlockSpec(memory_space=pl.ANY), vmem()),
+        out_specs=(vmem(), pl.BlockSpec(memory_space=pl.ANY)),
         scratch_shapes=[
-            pltpu.VMEM((raw_rows, ORDER), F32),
+            pltpu.VMEM((tiles, 2 * TILE, ORDER), F32),
             pltpu.SemaphoreType.DMA((tiles,)),
             pltpu.SemaphoreType.DMA((RAW_TILES,)),
         ],
@@ -218,9 +211,8 @@
     return jnp.concatenate([ref[tile_rows(2 * tile, TILE)], ref[tile_rows(2 * tile + 1, TILE)]], axis=1)
 
 
-def turn_kernel(flag_ref, rows_ref, x_ref, early_ref, late_ref, high, low):
+def turn_weights(rows_ref, is_back, high, low):
     front, back = rows_ref[:HALF], rows_ref[HALF:]
-    is_back = flag_ref[0] == 1
     early = jnp.where(is_back, back, front)
     late = jnp.where(is_back, front, back)
     none = jnp.zeros_like(early)
@@ -228,11 +220,54 @@
     lower = jnp.concatenate([none, early, none, late], axis=0)
     store_weights(jnp.concatenate([upper, lower], axis=1).T, high, low)
 
+
+def turn_tiles(x_ref, early_ref, late_ref, high, low):
     @pl.loop(0, early_ref.shape[0] // TILE, unroll=True)
     def _(tile):
         out = dot_three(packed(x_ref, tile), high, low)
         early_ref[tile_rows(tile, TILE)] = out[:, :ORDER]
         late_ref[tile_rows(tile, TILE)] = out[:, ORDER:]
+
+
+def turn_kernel(flag_ref, rows_ref, x_ref, early_ref, late_ref, high, low):
+    turn_weights(rows_ref, flag_ref[0] == 1, high, low)
+    turn_tiles(x_ref, early_ref, late_ref, high, low)
+
+
+def rotation_turn_kernel(flag_ref, gram_ref, x_ref, rows_ref, half_ref, early_ref, late_ref, high, low, held, sem):
+    first = x_ref.shape[0] - held.shape[0]
+    copy = pltpu.make_async_copy(x_ref.at[pl.ds(first, held.shape[0])], held, sem)
+    copy.start()
+    rotate(gram_ref[...], rows_ref)
+    is_back = flag_ref[0] == 1
+    half_ref[...] = jnp.where(is_back, rows_ref[:HALF], rows_ref[HALF:])
+    turn_weights(rows_ref, is_back, high, low)
+    copy.wait()
+    turn_tiles(held, early_ref, late_ref, high, low)
+
+
+def rotation_turn(flag, gram_total, columns):
+    rows = columns.shape[0] - RAW_TILES * 2 * TILE
+    half = jax.ShapeDtypeStruct((rows // 2, ORDER), F32)
+    return pl.pallas_call(
+        rotation_turn_kernel,
+        out_shape=(
+            jax.ShapeDtypeStruct((ORDER, ORDER), F32),
+            jax.ShapeDtypeStruct((HALF, ORDER), F32),
+            half,
+            half,
+        ),
+        in_specs=[smem(), vmem(), pl.BlockSpec(memory_space=pl.ANY)],
+        out_specs=(vmem(), vmem(), vmem(), vmem()),
+        scratch_shapes=[
+            pltpu.VMEM((2 * ORDER, 2 * ORDER), BF16),
+            pltpu.VMEM((2 * ORDER, 2 * ORDER), BF16),
+            pltpu.VMEM((rows, ORDER), F32),
+            pltpu.SemaphoreType.DMA,
+        ],
+        compiler_params=limit(ROTATION_LIMIT),
+        name="rotation_turn",
+    )(flag, gram_total, columns)
 
 
 def turn(columns, turn_rows, early_is_back):
@@ -421,7 +456,7 @@
 
 
 def summed(gram):
-    for by in (2, 4, 8):
+    for by in (2, 4, 14):
         gram = gram + moved(gram, swap_rows(by))
     return gram
 
@@ -440,13 +475,12 @@
     rest_tiles = tiles - RAW_TILES
     places = ((0, RAW_TILES), (RAW_TILES, rest_tiles))
 
-    gram, sent, rest = gram_and_rows(matrix)
+    gram, sent = gram_and_raw(matrix)
     raw_come = moved(sent, outward)
     gram = gram + moved(gram, swap_rows(1))
-    first_turn, half_turn = rotation_rows(flag, summed(gram), rest)
+    first_turn, half_turn, early_b, late_b = rotation_turn(flag, summed(gram), matrix)
     come_turn = moved(half_turn, inward_swapped)
 
-    early_b, late_b = turn(rest, first_turn, flag)
     come_b = moved(early_b, outward)
     early_a, late_a = turn(sent, tied(first_turn, early_b, come_turn), flag)
     come_a = turn_raw(raw_come, come_turn)
@@ -455,7 +489,7 @@
     last_a = moved(tied(late_a, second), inward)
     last_b = moved(tied(late_b, second), inward)
     second = second + moved(moved(second, swap_rows(1)), outward)
-    mine, _ = rotation_rows(flag, summed(second))
+    mine = rotation_rows(summed(second))
     other = moved(mine, swap_rows(1))
     flags = jnp.stack([early_is_back, core])
     parts = [early_a, late_a, come_a, last_a, early_b, late_b, come_b, last_b]

time: 121 us -> 114 us (0.942)
  starting transfers between devices: 44.9 us -> 40.5 us
  Pallas kernels: 41.8 us -> 39.6 us
  waiting for transfers between devices: 30.5 us -> 32.6 us
  local copies, waits for them, and re-layouts: 2.47 us -> 0.59 us
    ppermute x15, starting transfers between devices: 44.9 us -> 40.5 us  [moved(): return lax.ppermute(array, ('row', 'col'), pairs)]
    ppermute x15, waiting for transfers between devices: 30.5 us -> 32.6 us  [moved(): return lax.ppermute(array, ('row', 'col'), pairs)]
    unnamed x4 -> x2, local copies, waits for them, and re-layouts: 1.89 us -> 0.01 us
    pallas_call x2 -> x1, Pallas kernels: 4.91 us -> 3.38 us  [turn(): pl.pallas_call(turn_kernel, out_shape=(half, half), in_specs=[smem(), vme...]
  transfers between devices with their start and end apart: 15 -> 15, of which waited for: 12 -> 12; matrix products, arithmetic and copies ran while one was open for 1% -> 1% of each run, Pallas kernels for 24% -> 25%
where the time goes in v4:
time: 114 us
  starting transfers between devices  40.5 us (36%)
  Pallas kernels  39.6 us (35%)
  waiting for transfers between devices  32.6 us (29%)
    ppermute x15, starting transfers between devices, moved(): return lax.ppermute(array, ('row', 'col'), pairs)  40.5 us
    ppermute x15, waiting for transfers between devices, moved(): return lax.ppermute(array, ('row', 'col'), pairs)  32.6 us
    pallas_call x1, Pallas kernels, rotation_turn(): pl.pallas_call(rotation_turn_kernel, out_shape=(jax.ShapeDtypeStruct((ORD...  12.2 us
    pallas_call x1, Pallas kernels, rotation_rows(): pl.pallas_call(rotation_kernel, out_shape=jax.ShapeDtypeStruct((ORDER, OR...  10.6 us
    pallas_call x1, Pallas kernels, finish(): pl.pallas_call(functools.partial(finish_kernel, places), out_shape=jax.Sh...  5.34 us
    pallas_call x1, Pallas kernels, gram_and_raw(): pl.pallas_call(gram_kernel, out_shape=(jax.ShapeDtypeStruct((ORDER, ORDER...  4.54 us
    pallas_call x1, Pallas kernels, turn(): pl.pallas_call(turn_kernel, out_shape=(half, half), in_specs=[smem(), vme...  3.38 us
    pallas_call x2, Pallas kernels, pair_gram(): pl.pallas_call(pair_gram_kernel, out_shape=jax.ShapeDtypeStruct((ORDER, O...  2.46 us
  transfers between devices with their start and end apart: 15, of which 12 were waited for; matrix products, arithmetic and copies ran while one was open for 1% of the time, Pallas kernels for 25%

profile of v4, /device:TPU:1, one launch (start us, length us, event | category | flops | bytes accessed | tf_op | source)
XLA Modules:
  0.0 114.3 jit_solution(16790460671607386767)
XLA Ops:
  0.0 0.0 copy-start
  0.0 4.5 %gram.1 = (f32[128,128]{1,0:T(8,128)S(1)}, f32[6144,128]{1,0:T(8,128)}) custom-call(f32[12288,128]{1,0:T(8,128)} %x_ref.3), custom_call_target="tpu_custom_call" | custom-call | flops 805306368 | bytes 6291456 | tf_op jit(solution)/shard_map/gram/pallas_call | solution.py:176
  4.5 5.8 %collective-permute-start.5 = (f32[6144,128]{1,0:T(8,128)}, f32[6144,128]{1,0:T(8,128)S(1)}, u32[]{:S(2)}, u32[]{:S(2)}) collective-permute-start(f32[6144,128]{1,0:T(8,128)} %get-tuple-element.21.x_ref), channel_id=1, source_target_pairs={{0,1},{1,2},{2,3},{3,4},{4,5},{5,6},{6,7},{7,8},{8,9},{9,10},{10,1... | collective-permute-start | bytes 9437192 | tf_op jit(solution)/shard_map/ppermute | solution.py:438
  10.4 0.0 collective-permute-start
  10.4 1.3 %collective-permute-done = f32[128,128]{1,0:T(8,128)S(1)} collective-permute-done((f32[128,128]{1,0:T(8,128)S(1)}, f32[128,128]{1,0:T(8,128)S(1)}, u32[]{:S(2)}, u32[]{:S(2)}) %collective-permute-start) | collective-permute-done | bytes 65568 | tf_op jit(solution)/shard_map/ppermute | solution.py:438
  11.6 1.7 %collective-permute-start.1 = (f32[128,128]{1,0:T(8,128)S(1)}, f32[128,128]{1,0:T(8,128)S(1)}, u32[]{:S(2)}, u32[]{:S(2)}) collective-permute-start(f32[128,128]{1,0:T(8,128)S(1)} %add.33), channel_id=1, source_target_pairs={{0,32},{1,33},{2,34},{3,35},{4,36},{5,37},{6,38},{7,39},{8,40},{9,... | collective-permute-start | bytes 196616 | tf_op jit(solution)/shard_map/ppermute | solution.py:438
  13.4 2.3 %collective-permute-done.1 = f32[128,128]{1,0:T(8,128)S(1)} collective-permute-done((f32[128,128]{1,0:T(8,128)S(1)}, f32[128,128]{1,0:T(8,128)S(1)}, u32[]{:S(2)}, u32[]{:S(2)}) %collective-permute-start.1) | collective-permute-done | bytes 65568 | tf_op jit(solution)/shard_map/ppermute | solution.py:438
  15.7 3.1 %collective-permute-start.2 = (f32[128,128]{1,0:T(8,128)S(1)}, f32[128,128]{1,0:T(8,128)S(1)}, u32[]{:S(2)}, u32[]{:S(2)}) collective-permute-start(f32[128,128]{1,0:T(8,128)S(1)} %add.34), channel_id=1, source_target_pairs={{0,64},{1,65},{2,66},{3,67},{4,68},{5,69},{6,70},{7,71},{8,72},{9,... | collective-permute-start | bytes 196616 | tf_op jit(solution)/shard_map/ppermute | solution.py:438
  18.8 2.0 %collective-permute-done.2 = f32[128,128]{1,0:T(8,128)S(1)} collective-permute-done((f32[128,128]{1,0:T(8,128)S(1)}, f32[128,128]{1,0:T(8,128)S(1)}, u32[]{:S(2)}, u32[]{:S(2)}) %collective-permute-start.2) | collective-permute-done | bytes 65568 | tf_op jit(solution)/shard_map/ppermute | solution.py:438
  20.7 5.5 %collective-permute-start.3 = (f32[128,128]{1,0:T(8,128)S(1)}, f32[128,128]{1,0:T(8,128)S(1)}, u32[]{:S(2)}, u32[]{:S(2)}) collective-permute-start(f32[128,128]{1,0:T(8,128)S(1)} %add.35), channel_id=1, source_target_pairs={{0,224},{1,225},{2,226},{3,227},{4,228},{5,229},{6,230},{7,231},{8... | collective-permute-start | bytes 196616 | tf_op jit(solution)/shard_map/ppermute | solution.py:438
  26.3 0.0 copy-done
  26.3 0.6 dynamic_slice.3
  27.4 1.2 %collective-permute-done.3 = f32[128,128]{1,0:T(8,128)S(1)} collective-permute-done((f32[128,128]{1,0:T(8,128)S(1)}, f32[128,128]{1,0:T(8,128)S(1)}, u32[]{:S(2)}, u32[]{:S(2)}) %collective-permute-start.3) | collective-permute-done | bytes 65568 | tf_op jit(solution)/shard_map/ppermute | solution.py:438
  28.7 12.2 %rotation_turn.1 = (f32[128,128]{1,0:T(8,128)S(1)}, f32[64,128]{1,0:T(8,128)S(1)}, f32[3072,128]{1,0:T(8,128)S(1)}, f32[3072,128]{1,0:T(8,128)S(1)}) custom-call(s32[1]{0:T(128)} %bitcast.1.flag_ref, f32[128,128]{1,0:T(8,128)S(1)} %add.36.gram_ref, f32[12288,128]{1,0:T(8,128)} %x_ref.3), custom_call_target="tpu_custom_call" | custom-call | tf_op jit(solution)/shard_map/rotation_turn/pallas_call | solution.py:252
  40.9 0.1 collective-permute-start.6
  40.9 1.8 %collective-permute-start.4 = (f32[64,128]{1,0:T(8,128)S(1)}, f32[64,128]{1,0:T(8,128)S(1)}, u32[]{:S(2)}, u32[]{:S(2)}) collective-permute-start(f32[64,128]{1,0:T(8,128)S(1)} %get-tuple-element.19), channel_id=1, source_target_pairs={{0,31},{1,16},{2,17},{3,18},{4,19},{5,20},{6,21},{7,22},{8,23},{9,... | collective-permute-start | bytes 98312 | tf_op jit(solution)/shard_map/ppermute | solution.py:438
  42.7 2.5 %collective-permute-done.4.rows_ref = f32[64,128]{1,0:T(8,128)S(1)} collective-permute-done((f32[64,128]{1,0:T(8,128)S(1)}, f32[64,128]{1,0:T(8,128)S(1)}, u32[]{:S(2)}, u32[]{:S(2)}) %collective-permute-start.4) | collective-permute-done | bytes 32800 | tf_op jit(solution)/shard_map/ppermute | solution.py:438
  45.2 3.4 %turn.1 = (f32[3072,128]{1,0:T(8,128)S(1)}, f32[3072,128]{1,0:T(8,128)S(1)}) custom-call(s32[1]{0:T(128)} %bitcast.1.flag_ref, f32[128,128]{1,0:T(8,128)S(1)} %get-tuple-element.20.rows_ref, f32[6144,128]{1,0:T(8,128)} %get-tuple-element.21.x_ref), custom_call_target="tpu_custom_call" | custom-call | flops 1207959552 | bytes 6291456 | tf_op jit(solution)/shard_map/turn/pallas_call | solution.py:275
  48.6 0.0 collective-permute-done.5.x_ref
  48.6 1.1 turn_raw.1.come_ref.refs_2_
  49.7 1.2 %pair_gram.2.before_ref = f32[128,128]{1,0:T(8,128)S(1)} custom-call(s32[1]{0:T(128)} %bitcast.2.core_ref, f32[128,128]{1,0:T(8,128)S(1)} %broadcast_in_dim.3.before_ref, f32[3072,128]{1,0:T(8,128)S(1)} %get-tuple-element.25.own_ref.refs_1_, f32[3072,128]{1,0:T(8,128)S(1)} %turn_raw.1.come_ref.refs_2_), custom_call_target="tpu_custom_call" | custom-call | flops 805306368 | bytes 3145728 | tf_op jit(solution)/shard_map/pair_gram/pallas_call | solution.py:342
  51.0 11.1 %collective-permute-done.6.come_ref.refs_6_ = f32[3072,128]{1,0:T(8,128)S(1)} collective-permute-done((f32[3072,128]{1,0:T(8,128)S(1)}, f32[3072,128]{1,0:T(8,128)S(1)}, u32[]{:S(2)}, u32[]{:S(2)}) %collective-permute-start.6) | collective-permute-done | bytes 1572896 | tf_op jit(solution)/shard_map/ppermute | solution.py:438
  62.0 1.2 %pair_gram.3 = f32[128,128]{1,0:T(8,128)S(1)} custom-call(s32[1]{0:T(128)} %bitcast.2.core_ref, f32[128,128]{1,0:T(8,128)S(1)} %pair_gram.2.before_ref, f32[3072,128]{1,0:T(8,128)S(1)} %get-tuple-element.26.own_ref.refs_5_, f32[3072,128]{1,0:T(8,128)S(1)} %collective-permute-done.6.come_ref.refs_6_), custom_call_target="tpu_custom_call" | custom-call | flops 805306368 | bytes 3145728 | tf_op jit(solution)/shard_map/pair_gram/pallas_call | solution.py:342
  63.3 0.1 collective-permute-start.13
  63.3 0.1 collective-permute-start.14
  63.4 5.3 %collective-permute-start.7 = (f32[128,128]{1,0:T(8,128)S(1)}, f32[128,128]{1,0:T(8,128)S(1)}, u32[]{:S(2)}, u32[]{:S(2)}) collective-permute-start(f32[128,128]{1,0:T(8,128)S(1)} %pair_gram.3), channel_id=1, source_target_pairs={{0,16},{1,17},{2,18},{3,19},{4,20},{5,21},{6,22},{7,23},{8,24},{9,... | collective-permute-start | bytes 196616 | tf_op jit(solution)/shard_map/ppermute | solution.py:438
  68.8 0.9 collective-permute-done.7
  69.7 0.3 collective-permute-start.8
  70.0 3.9 %collective-permute-done.8 = f32[128,128]{1,0:T(8,128)S(1)} collective-permute-done((f32[128,128]{1,0:T(8,128)S(1)}, f32[128,128]{1,0:T(8,128)S(1)}, u32[]{:S(2)}, u32[]{:S(2)}) %collective-permute-start.8) | collective-permute-done | bytes 65568 | tf_op jit(solution)/shard_map/ppermute | solution.py:438
  74.0 1.0 collective-permute-start.9
  74.9 2.5 %collective-permute-done.9 = f32[128,128]{1,0:T(8,128)S(1)} collective-permute-done((f32[128,128]{1,0:T(8,128)S(1)}, f32[128,128]{1,0:T(8,128)S(1)}, u32[]{:S(2)}, u32[]{:S(2)}) %collective-permute-start.9) | collective-permute-done | bytes 65568 | tf_op jit(solution)/shard_map/ppermute | solution.py:438
  77.5 2.6 %collective-permute-start.10 = (f32[128,128]{1,0:T(8,128)S(1)}, f32[128,128]{1,0:T(8,128)S(1)}, u32[]{:S(2)}, u32[]{:S(2)}) collective-permute-start(f32[128,128]{1,0:T(8,128)S(1)} %add.38), channel_id=1, source_target_pairs={{0,64},{1,65},{2,66},{3,67},{4,68},{5,69},{6,70},{7,71},{8,72},{9,... | collective-permute-start | bytes 196616 | tf_op jit(solution)/shard_map/ppermute | solution.py:438
  80.0 1.9 %collective-permute-done.10 = f32[128,128]{1,0:T(8,128)S(1)} collective-permute-done((f32[128,128]{1,0:T(8,128)S(1)}, f32[128,128]{1,0:T(8,128)S(1)}, u32[]{:S(2)}, u32[]{:S(2)}) %collective-permute-start.10) | collective-permute-done | bytes 65568 | tf_op jit(solution)/shard_map/ppermute | solution.py:438
  82.0 5.6 %collective-permute-start.11 = (f32[128,128]{1,0:T(8,128)S(1)}, f32[128,128]{1,0:T(8,128)S(1)}, u32[]{:S(2)}, u32[]{:S(2)}) collective-permute-start(f32[128,128]{1,0:T(8,128)S(1)} %add.39), channel_id=1, source_target_pairs={{0,224},{1,225},{2,226},{3,227},{4,228},{5,229},{6,230},{7,231},{8... | collective-permute-start | bytes 196616 | tf_op jit(solution)/shard_map/ppermute | solution.py:438
  87.5 2.2 %collective-permute-done.11 = f32[128,128]{1,0:T(8,128)S(1)} collective-permute-done((f32[128,128]{1,0:T(8,128)S(1)}, f32[128,128]{1,0:T(8,128)S(1)}, u32[]{:S(2)}, u32[]{:S(2)}) %collective-permute-start.11) | collective-permute-done | bytes 65568 | tf_op jit(solution)/shard_map/ppermute | solution.py:438
  89.7 10.6 %rotation.1.mine_ref = f32[128,128]{1,0:T(8,128)S(1)} custom-call(f32[128,128]{1,0:T(8,128)S(1)} %add.40.gram_ref), custom_call_target="tpu_custom_call" | custom-call | tf_op jit(solution)/shard_map/rotation/pallas_call | solution.py:120
  100.4 7.5 %collective-permute-start.12 = (f32[128,128]{1,0:T(8,128)S(1)}, f32[128,128]{1,0:T(8,128)S(1)}, u32[]{:S(2)}, u32[]{:S(2)}) collective-permute-start(f32[128,128]{1,0:T(8,128)S(1)} %rotation.1.mine_ref), channel_id=1, source_target_pairs={{0,16},{1,17},{2,18},{3,19},{4,20},{5,21},{6,22},{7,23},{8,24},{9,... | collective-permute-start | bytes 196616 | tf_op jit(solution)/shard_map/ppermute | solution.py:438
  107.8 0.1 pad_add_fusion.flags_ref
  107.9 0.8 collective-permute-done.12.other_ref
  108.7 0.0 collective-permute-done.13.refs_3_
  108.7 0.0 collective-permute-done.14.refs_7_
  108.8 5.3 %finish.1 = f32[12288,128]{1,0:T(8,128)} custom-call(s32[2]{0:T(128)S(1)} %pad_add_fusion.flags_ref, f32[128,128]{1,0:T(8,128)S(1)} %rotation.1.mine_ref, f32[128,128]{1,0:T(8,128)S(1)} %collective-permute-done.12.other_ref, f32[3072,128]{1,0:T(8,128)S(1)} %get-tuple-element.24.refs_0_, f32[3072,128]{1,0:T(8,128)S(1)} %get-tuple-element.25.own_ref.refs_1_, ...), custom_call_target="tpu_custom_call" | custom-call | tf_op jit(solution)/shard_map/finish/pallas_call | solution.py:413
  (9 shorter events, 0.1 us)
Async XLA Ops:
  0.0 26.3 %copy-start = (s32[16]{0:T(128)S(1)}, s32[16]{0:T(128)}, u32[]{:S(2)}) copy-start(s32[16]{0:T(128)} %param.3) | copy-start | bytes 196
  4.5 44.1 %collective-permute-start.5 = (f32[6144,128]{1,0:T(8,128)}, f32[6144,128]{1,0:T(8,128)S(1)}, u32[]{:S(2)}, u32[]{:S(2)}) collective-permute-start(f32[6144,128]{1,0:T(8,128)} %get-tuple-element.21.x_ref), channel_id=1, source_target_pairs={{0,1},{1,2},{2,3},{3,4},{4,5},{5,6},{6,7},{7,8},{8,9},{9,10},{10,1... | collective-permute-start | bytes 9437192 | tf_op jit(solution)/shard_map/ppermute | solution.py:438
  10.4 1.3 %collective-permute-start = (f32[128,128]{1,0:T(8,128)S(1)}, f32[128,128]{1,0:T(8,128)S(1)}, u32[]{:S(2)}, u32[]{:S(2)}) collective-permute-start(f32[128,128]{1,0:T(8,128)S(1)} %get-tuple-element.16), channel_id=1, source_target_pairs={{0,16},{1,17},{2,18},{3,19},{4,20},{5,21},{6,22},{7,23},{8,24},{9,... | collective-permute-start | bytes 196616 | tf_op jit(solution)/shard_map/ppermute | solution.py:438
  11.6 4.0 %collective-permute-start.1 = (f32[128,128]{1,0:T(8,128)S(1)}, f32[128,128]{1,0:T(8,128)S(1)}, u32[]{:S(2)}, u32[]{:S(2)}) collective-permute-start(f32[128,128]{1,0:T(8,128)S(1)} %add.33), channel_id=1, source_target_pairs={{0,32},{1,33},{2,34},{3,35},{4,36},{5,37},{6,38},{7,39},{8,40},{9,... | collective-permute-start | bytes 196616 | tf_op jit(solution)/shard_map/ppermute | solution.py:438
  15.7 5.0 %collective-permute-start.2 = (f32[128,128]{1,0:T(8,128)S(1)}, f32[128,128]{1,0:T(8,128)S(1)}, u32[]{:S(2)}, u32[]{:S(2)}) collective-permute-start(f32[128,128]{1,0:T(8,128)S(1)} %add.34), channel_id=1, source_target_pairs={{0,64},{1,65},{2,66},{3,67},{4,68},{5,69},{6,70},{7,71},{8,72},{9,... | collective-permute-start | bytes 196616 | tf_op jit(solution)/shard_map/ppermute | solution.py:438
  20.7 7.9 %collective-permute-start.3 = (f32[128,128]{1,0:T(8,128)S(1)}, f32[128,128]{1,0:T(8,128)S(1)}, u32[]{:S(2)}, u32[]{:S(2)}) collective-permute-start(f32[128,128]{1,0:T(8,128)S(1)} %add.35), channel_id=1, source_target_pairs={{0,224},{1,225},{2,226},{3,227},{4,228},{5,229},{6,230},{7,231},{8... | collective-permute-start | bytes 196616 | tf_op jit(solution)/shard_map/ppermute | solution.py:438
  40.9 21.2 %collective-permute-start.6 = (f32[3072,128]{1,0:T(8,128)S(1)}, f32[3072,128]{1,0:T(8,128)S(1)}, u32[]{:S(2)}, u32[]{:S(2)}) collective-permute-start(f32[3072,128]{1,0:T(8,128)S(1)} %get-tuple-element.18.refs_4_), channel_id=1, source_target_pairs={{0,1},{1,2},{2,3},{3,4},{4,5},{5,6},{6,7},{7,8},{8,9},{9,10},{10,1... | collective-permute-start | bytes 4718600 | tf_op jit(solution)/shard_map/ppermute | solution.py:438
  40.9 4.3 %collective-permute-start.4 = (f32[64,128]{1,0:T(8,128)S(1)}, f32[64,128]{1,0:T(8,128)S(1)}, u32[]{:S(2)}, u32[]{:S(2)}) collective-permute-start(f32[64,128]{1,0:T(8,128)S(1)} %get-tuple-element.19), channel_id=1, source_target_pairs={{0,31},{1,16},{2,17},{3,18},{4,19},{5,20},{6,21},{7,22},{8,23},{9,... | collective-permute-start | bytes 98312 | tf_op jit(solution)/shard_map/ppermute | solution.py:438
  63.3 45.5 %collective-permute-start.13 = (f32[3072,128]{1,0:T(8,128)S(1)}, f32[3072,128]{1,0:T(8,128)S(1)}, u32[]{:S(2)}, u32[]{:S(2)}) collective-permute-start(f32[3072,128]{1,0:T(8,128)S(1)} %get-tuple-element.25.own_ref.refs_1_), channel_id=1, source_target_pairs={{0,15},{1,0},{2,1},{3,2},{4,3},{5,4},{6,5},{7,6},{8,7},{9,8},{10,9... | collective-permute-start | bytes 4718600 | tf_op jit(solution)/shard_map/ppermute | solution.py:438
  63.3 45.4 %collective-permute-start.14 = (f32[3072,128]{1,0:T(8,128)S(1)}, f32[3072,128]{1,0:T(8,128)S(1)}, u32[]{:S(2)}, u32[]{:S(2)}) collective-permute-start(f32[3072,128]{1,0:T(8,128)S(1)} %get-tuple-element.26.own_ref.refs_5_), channel_id=1, source_target_pairs={{0,15},{1,0},{2,1},{3,2},{4,3},{5,4},{6,5},{7,6},{8,7},{9,8},{10,9... | collective-permute-start | bytes 4718600 | tf_op jit(solution)/shard_map/ppermute | solution.py:438
  63.4 6.2 %collective-permute-start.7 = (f32[128,128]{1,0:T(8,128)S(1)}, f32[128,128]{1,0:T(8,128)S(1)}, u32[]{:S(2)}, u32[]{:S(2)}) collective-permute-start(f32[128,128]{1,0:T(8,128)S(1)} %pair_gram.3), channel_id=1, source_target_pairs={{0,16},{1,17},{2,18},{3,19},{4,20},{5,21},{6,22},{7,23},{8,24},{9,... | collective-permute-start | bytes 196616 | tf_op jit(solution)/shard_map/ppermute | solution.py:438
  69.7 4.3 %collective-permute-start.8 = (f32[128,128]{1,0:T(8,128)S(1)}, f32[128,128]{1,0:T(8,128)S(1)}, u32[]{:S(2)}, u32[]{:S(2)}) collective-permute-start(f32[128,128]{1,0:T(8,128)S(1)} %collective-permute-done.7), channel_id=1, source_target_pairs={{0,1},{1,2},{2,3},{3,4},{4,5},{5,6},{6,7},{7,8},{8,9},{9,10},{10,1... | collective-permute-start | bytes 196616 | tf_op jit(solution)/shard_map/ppermute | solution.py:438
  74.0 3.5 %collective-permute-start.9 = (f32[128,128]{1,0:T(8,128)S(1)}, f32[128,128]{1,0:T(8,128)S(1)}, u32[]{:S(2)}, u32[]{:S(2)}) collective-permute-start(f32[128,128]{1,0:T(8,128)S(1)} %add.37), channel_id=1, source_target_pairs={{0,32},{1,33},{2,34},{3,35},{4,36},{5,37},{6,38},{7,39},{8,40},{9,... | collective-permute-start | bytes 196616 | tf_op jit(solution)/shard_map/ppermute | solution.py:438
  77.5 4.5 %collective-permute-start.10 = (f32[128,128]{1,0:T(8,128)S(1)}, f32[128,128]{1,0:T(8,128)S(1)}, u32[]{:S(2)}, u32[]{:S(2)}) collective-permute-start(f32[128,128]{1,0:T(8,128)S(1)} %add.38), channel_id=1, source_target_pairs={{0,64},{1,65},{2,66},{3,67},{4,68},{5,69},{6,70},{7,71},{8,72},{9,... | collective-permute-start | bytes 196616 | tf_op jit(solution)/shard_map/ppermute | solution.py:438
  82.0 7.8 %collective-permute-start.11 = (f32[128,128]{1,0:T(8,128)S(1)}, f32[128,128]{1,0:T(8,128)S(1)}, u32[]{:S(2)}, u32[]{:S(2)}) collective-permute-start(f32[128,128]{1,0:T(8,128)S(1)} %add.39), channel_id=1, source_target_pairs={{0,224},{1,225},{2,226},{3,227},{4,228},{5,229},{6,230},{7,231},{8... | collective-permute-start | bytes 196616 | tf_op jit(solution)/shard_map/ppermute | solution.py:438
  100.4 8.4 %collective-permute-start.12 = (f32[128,128]{1,0:T(8,128)S(1)}, f32[128,128]{1,0:T(8,128)S(1)}, u32[]{:S(2)}, u32[]{:S(2)}) collective-permute-start(f32[128,128]{1,0:T(8,128)S(1)} %rotation.1.mine_ref), channel_id=1, source_target_pairs={{0,16},{1,17},{2,18},{3,19},{4,20},{5,21},{6,22},{7,23},{8,24},{9,... | collective-permute-start | bytes 196616 | tf_op jit(solution)/shard_map/ppermute | solution.py:438

commit v5 on v4

--- a/solution.py
+++ b/solution.py
@@ -11,8 +11,8 @@
 ORDER = 128
 HALF = 64
 GROUP = 8
-TILE = 512
-RAW_TILES = 6
+TILE = 256
+RAW_TILES = 11
 GRAM_LIMIT = 48
 ROTATION_LIMIT = 48
 F32 = jnp.float32
@@ -485,9 +485,9 @@
     early_a, late_a = turn(sent, tied(first_turn, early_b, come_turn), flag)
     come_a = turn_raw(raw_come, come_turn)
     second = pair_gram(core_flag, jnp.zeros_like(gram), late_a, come_a)
+    last_a = moved(tied(late_a, second, come_b), inward)
+    last_b = moved(tied(late_b, second, come_b), inward)
     second = pair_gram(core_flag, second, late_b, come_b)
-    last_a = moved(tied(late_a, second), inward)
-    last_b = moved(tied(late_b, second), inward)
     second = second + moved(moved(second, swap_rows(1)), outward)
     mine = rotation_rows(summed(second))
     other = moved(mine, swap_rows(1))

time: 114 us -> 114 us (level)
  starting transfers between devices: 40.5 us -> 37.3 us
  waiting for transfers between devices: 32.6 us -> 34.8 us
    ppermute x15, starting transfers between devices: 40.5 us -> 37.3 us  [moved(): return lax.ppermute(array, ('row', 'col'), pairs)]
    ppermute x15, waiting for transfers between devices: 32.6 us -> 34.8 us  [moved(): return lax.ppermute(array, ('row', 'col'), pairs)]
  transfers between devices with their start and end apart: 15 -> 15, of which waited for: 12 -> 12; matrix products, arithmetic and copies ran while one was open for 1% -> 1% of each run, Pallas kernels for 25% -> 26%
where the time goes in v5:
time: 114 us; the launch traced here: 113 us
  Pallas kernels  39.7 us (35%)
  starting transfers between devices  37.3 us (33%)
  waiting for transfers between devices  34.8 us (31%)
    ppermute x15, starting transfers between devices, moved(): return lax.ppermute(array, ('row', 'col'), pairs)  37.3 us
    ppermute x15, waiting for transfers between devices, moved(): return lax.ppermute(array, ('row', 'col'), pairs)  34.8 us
    pallas_call x1, Pallas kernels, rotation_turn(): pl.pallas_call(rotation_turn_kernel, out_shape=(jax.ShapeDtypeStruct((ORD...  12.3 us
    pallas_call x1, Pallas kernels, rotation_rows(): pl.pallas_call(rotation_kernel, out_shape=jax.ShapeDtypeStruct((ORDER, OR...  10.6 us
    pallas_call x1, Pallas kernels, finish(): pl.pallas_call(functools.partial(finish_kernel, places), out_shape=jax.Sh...  5.37 us
    pallas_call x1, Pallas kernels, gram_and_raw(): pl.pallas_call(gram_kernel, out_shape=(jax.ShapeDtypeStruct((ORDER, ORDER...  4.76 us
    pallas_call x1, Pallas kernels, turn(): pl.pallas_call(turn_kernel, out_shape=(half, half), in_specs=[smem(), vme...  3.21 us
    pallas_call x2, Pallas kernels, pair_gram(): pl.pallas_call(pair_gram_kernel, out_shape=jax.ShapeDtypeStruct((ORDER, O...  2.45 us
  transfers between devices with their start and end apart: 15, of which 12 were waited for; matrix products, arithmetic and copies ran while one was open for 1% of the time, Pallas kernels for 26%

profile of v5, /device:TPU:1, one launch (start us, length us, event | category | flops | bytes accessed | tf_op | source)
XLA Modules:
  0.0 113.4 jit_solution(15089324486383252306)
XLA Ops:
  0.0 0.0 copy-start
  0.0 4.8 %gram.1 = (f32[128,128]{1,0:T(8,128)S(1)}, f32[5632,128]{1,0:T(8,128)}) custom-call(f32[12288,128]{1,0:T(8,128)} %x_ref.3), custom_call_target="tpu_custom_call" | custom-call | flops 805306368 | bytes 6291456 | tf_op jit(solution)/shard_map/gram/pallas_call | solution.py:176
  4.8 5.8 %collective-permute-start.5 = (f32[5632,128]{1,0:T(8,128)}, f32[5632,128]{1,0:T(8,128)S(1)}, u32[]{:S(2)}, u32[]{:S(2)}) collective-permute-start(f32[5632,128]{1,0:T(8,128)} %get-tuple-element.21.x_ref), channel_id=1, source_target_pairs={{0,1},{1,2},{2,3},{3,4},{4,5},{5,6},{6,7},{7,8},{8,9},{9,10},{10,1... | collective-permute-start | bytes 8650760 | tf_op jit(solution)/shard_map/ppermute | solution.py:438
  10.6 0.0 collective-permute-start
  10.6 1.3 %collective-permute-done = f32[128,128]{1,0:T(8,128)S(1)} collective-permute-done((f32[128,128]{1,0:T(8,128)S(1)}, f32[128,128]{1,0:T(8,128)S(1)}, u32[]{:S(2)}, u32[]{:S(2)}) %collective-permute-start) | collective-permute-done | bytes 65568 | tf_op jit(solution)/shard_map/ppermute | solution.py:438
  11.9 1.7 %collective-permute-start.1 = (f32[128,128]{1,0:T(8,128)S(1)}, f32[128,128]{1,0:T(8,128)S(1)}, u32[]{:S(2)}, u32[]{:S(2)}) collective-permute-start(f32[128,128]{1,0:T(8,128)S(1)} %add.33), channel_id=1, source_target_pairs={{0,32},{1,33},{2,34},{3,35},{4,36},{5,37},{6,38},{7,39},{8,40},{9,... | collective-permute-start | bytes 196616 | tf_op jit(solution)/shard_map/ppermute | solution.py:438
  13.6 2.3 %collective-permute-done.1 = f32[128,128]{1,0:T(8,128)S(1)} collective-permute-done((f32[128,128]{1,0:T(8,128)S(1)}, f32[128,128]{1,0:T(8,128)S(1)}, u32[]{:S(2)}, u32[]{:S(2)}) %collective-permute-start.1) | collective-permute-done | bytes 65568 | tf_op jit(solution)/shard_map/ppermute | solution.py:438
  15.9 3.1 %collective-permute-start.2 = (f32[128,128]{1,0:T(8,128)S(1)}, f32[128,128]{1,0:T(8,128)S(1)}, u32[]{:S(2)}, u32[]{:S(2)}) collective-permute-start(f32[128,128]{1,0:T(8,128)S(1)} %add.34), channel_id=1, source_target_pairs={{0,64},{1,65},{2,66},{3,67},{4,68},{5,69},{6,70},{7,71},{8,72},{9,... | collective-permute-start | bytes 196616 | tf_op jit(solution)/shard_map/ppermute | solution.py:438
  19.0 2.0 %collective-permute-done.2 = f32[128,128]{1,0:T(8,128)S(1)} collective-permute-done((f32[128,128]{1,0:T(8,128)S(1)}, f32[128,128]{1,0:T(8,128)S(1)}, u32[]{:S(2)}, u32[]{:S(2)}) %collective-permute-start.2) | collective-permute-done | bytes 65568 | tf_op jit(solution)/shard_map/ppermute | solution.py:438
  20.9 5.5 %collective-permute-start.3 = (f32[128,128]{1,0:T(8,128)S(1)}, f32[128,128]{1,0:T(8,128)S(1)}, u32[]{:S(2)}, u32[]{:S(2)}) collective-permute-start(f32[128,128]{1,0:T(8,128)S(1)} %add.35), channel_id=1, source_target_pairs={{0,224},{1,225},{2,226},{3,227},{4,228},{5,229},{6,230},{7,231},{8... | collective-permute-start | bytes 196616 | tf_op jit(solution)/shard_map/ppermute | solution.py:438
  26.5 0.0 copy-done
  26.5 0.6 dynamic_slice.3
  27.6 1.2 %collective-permute-done.3 = f32[128,128]{1,0:T(8,128)S(1)} collective-permute-done((f32[128,128]{1,0:T(8,128)S(1)}, f32[128,128]{1,0:T(8,128)S(1)}, u32[]{:S(2)}, u32[]{:S(2)}) %collective-permute-start.3) | collective-permute-done | bytes 65568 | tf_op jit(solution)/shard_map/ppermute | solution.py:438
  28.9 12.3 %rotation_turn.1 = (f32[128,128]{1,0:T(8,128)S(1)}, f32[64,128]{1,0:T(8,128)S(1)}, f32[3328,128]{1,0:T(8,128)S(1)}, f32[3328,128]{1,0:T(8,128)S(1)}) custom-call(s32[1]{0:T(128)} %bitcast.1.flag_ref, f32[128,128]{1,0:T(8,128)S(1)} %add.36.gram_ref, f32[12288,128]{1,0:T(8,128)} %x_ref.3), custom_call_target="tpu_custom_call" | custom-call | tf_op jit(solution)/shard_map/rotation_turn/pallas_call | solution.py:252
  41.2 0.1 collective-permute-start.6
  41.3 1.8 %collective-permute-start.4 = (f32[64,128]{1,0:T(8,128)S(1)}, f32[64,128]{1,0:T(8,128)S(1)}, u32[]{:S(2)}, u32[]{:S(2)}) collective-permute-start(f32[64,128]{1,0:T(8,128)S(1)} %get-tuple-element.19), channel_id=1, source_target_pairs={{0,31},{1,16},{2,17},{3,18},{4,19},{5,20},{6,21},{7,22},{8,23},{9,... | collective-permute-start | bytes 98312 | tf_op jit(solution)/shard_map/ppermute | solution.py:438
  43.0 2.3 %collective-permute-done.4.rows_ref = f32[64,128]{1,0:T(8,128)S(1)} collective-permute-done((f32[64,128]{1,0:T(8,128)S(1)}, f32[64,128]{1,0:T(8,128)S(1)}, u32[]{:S(2)}, u32[]{:S(2)}) %collective-permute-start.4) | collective-permute-done | bytes 32800 | tf_op jit(solution)/shard_map/ppermute | solution.py:438
  45.3 3.2 %turn.1 = (f32[2816,128]{1,0:T(8,128)S(1)}, f32[2816,128]{1,0:T(8,128)S(1)}) custom-call(s32[1]{0:T(128)} %bitcast.1.flag_ref, f32[128,128]{1,0:T(8,128)S(1)} %get-tuple-element.20.rows_ref, f32[5632,128]{1,0:T(8,128)} %get-tuple-element.21.x_ref), custom_call_target="tpu_custom_call" | custom-call | flops 1107296256 | bytes 5767168 | tf_op jit(solution)/shard_map/turn/pallas_call | solution.py:275
  48.5 0.0 collective-permute-done.5.x_ref
  48.5 1.0 turn_raw.1.come_ref.refs_2_
  49.5 1.1 %pair_gram.2.before_ref = f32[128,128]{1,0:T(8,128)S(1)} custom-call(s32[1]{0:T(128)} %bitcast.2.core_ref, f32[128,128]{1,0:T(8,128)S(1)} %broadcast_in_dim.3.before_ref, f32[2816,128]{1,0:T(8,128)S(1)} %get-tuple-element.25.own_ref.refs_1_, f32[2816,128]{1,0:T(8,128)S(1)} %turn_raw.1.come_ref.refs_2_), custom_call_target="tpu_custom_call" | custom-call | flops 738197504 | bytes 2883584 | tf_op jit(solution)/shard_map/pair_gram/pallas_call | solution.py:342
  50.7 11.9 %collective-permute-done.6.come_ref.refs_6_ = f32[3328,128]{1,0:T(8,128)S(1)} collective-permute-done((f32[3328,128]{1,0:T(8,128)S(1)}, f32[3328,128]{1,0:T(8,128)S(1)}, u32[]{:S(2)}, u32[]{:S(2)}) %collective-permute-start.6) | collective-permute-done | bytes 1703968 | tf_op jit(solution)/shard_map/ppermute | solution.py:438
  62.6 0.0 collective-permute-start.14
  62.6 0.0 collective-permute-start.13
  62.6 1.3 %pair_gram.3 = f32[128,128]{1,0:T(8,128)S(1)} custom-call(s32[1]{0:T(128)} %bitcast.2.core_ref, f32[128,128]{1,0:T(8,128)S(1)} %pair_gram.2.before_ref, f32[3328,128]{1,0:T(8,128)S(1)} %get-tuple-element.26.own_ref.refs_5_, f32[3328,128]{1,0:T(8,128)S(1)} %collective-permute-done.6.come_ref.refs_6_), custom_call_target="tpu_custom_call" | custom-call | flops 872415232 | bytes 3407872 | tf_op jit(solution)/shard_map/pair_gram/pallas_call | solution.py:342
  63.9 6.4 %collective-permute-start.7 = (f32[128,128]{1,0:T(8,128)S(1)}, f32[128,128]{1,0:T(8,128)S(1)}, u32[]{:S(2)}, u32[]{:S(2)}) collective-permute-start(f32[128,128]{1,0:T(8,128)S(1)} %pair_gram.3), channel_id=1, source_target_pairs={{0,16},{1,17},{2,18},{3,19},{4,20},{5,21},{6,22},{7,23},{8,24},{9,... | collective-permute-start | bytes 196616 | tf_op jit(solution)/shard_map/ppermute | solution.py:438
  70.3 0.9 collective-permute-done.7
  71.2 1.0 collective-permute-start.8
  72.2 3.5 %collective-permute-done.8 = f32[128,128]{1,0:T(8,128)S(1)} collective-permute-done((f32[128,128]{1,0:T(8,128)S(1)}, f32[128,128]{1,0:T(8,128)S(1)}, u32[]{:S(2)}, u32[]{:S(2)}) %collective-permute-start.8) | collective-permute-done | bytes 65568 | tf_op jit(solution)/shard_map/ppermute | solution.py:438
  75.7 0.6 collective-permute-start.9
  76.3 2.9 %collective-permute-done.9 = f32[128,128]{1,0:T(8,128)S(1)} collective-permute-done((f32[128,128]{1,0:T(8,128)S(1)}, f32[128,128]{1,0:T(8,128)S(1)}, u32[]{:S(2)}, u32[]{:S(2)}) %collective-permute-start.9) | collective-permute-done | bytes 65568 | tf_op jit(solution)/shard_map/ppermute | solution.py:438
  79.2 1.3 %collective-permute-start.10 = (f32[128,128]{1,0:T(8,128)S(1)}, f32[128,128]{1,0:T(8,128)S(1)}, u32[]{:S(2)}, u32[]{:S(2)}) collective-permute-start(f32[128,128]{1,0:T(8,128)S(1)} %add.38), channel_id=1, source_target_pairs={{0,64},{1,65},{2,66},{3,67},{4,68},{5,69},{6,70},{7,71},{8,72},{9,... | collective-permute-start | bytes 196616 | tf_op jit(solution)/shard_map/ppermute | solution.py:438
  80.5 3.5 %collective-permute-done.10 = f32[128,128]{1,0:T(8,128)S(1)} collective-permute-done((f32[128,128]{1,0:T(8,128)S(1)}, f32[128,128]{1,0:T(8,128)S(1)}, u32[]{:S(2)}, u32[]{:S(2)}) %collective-permute-start.10) | collective-permute-done | bytes 65568 | tf_op jit(solution)/shard_map/ppermute | solution.py:438
  84.0 2.3 %collective-permute-start.11 = (f32[128,128]{1,0:T(8,128)S(1)}, f32[128,128]{1,0:T(8,128)S(1)}, u32[]{:S(2)}, u32[]{:S(2)}) collective-permute-start(f32[128,128]{1,0:T(8,128)S(1)} %add.39), channel_id=1, source_target_pairs={{0,224},{1,225},{2,226},{3,227},{4,228},{5,229},{6,230},{7,231},{8... | collective-permute-start | bytes 196616 | tf_op jit(solution)/shard_map/ppermute | solution.py:438
  86.4 2.2 %collective-permute-done.11 = f32[128,128]{1,0:T(8,128)S(1)} collective-permute-done((f32[128,128]{1,0:T(8,128)S(1)}, f32[128,128]{1,0:T(8,128)S(1)}, u32[]{:S(2)}, u32[]{:S(2)}) %collective-permute-start.11) | collective-permute-done | bytes 65568 | tf_op jit(solution)/shard_map/ppermute | solution.py:438
  88.6 10.6 %rotation.1.mine_ref = f32[128,128]{1,0:T(8,128)S(1)} custom-call(f32[128,128]{1,0:T(8,128)S(1)} %add.40.gram_ref), custom_call_target="tpu_custom_call" | custom-call | tf_op jit(solution)/shard_map/rotation/pallas_call | solution.py:120
  99.2 7.7 %collective-permute-start.12 = (f32[128,128]{1,0:T(8,128)S(1)}, f32[128,128]{1,0:T(8,128)S(1)}, u32[]{:S(2)}, u32[]{:S(2)}) collective-permute-start(f32[128,128]{1,0:T(8,128)S(1)} %rotation.1.mine_ref), channel_id=1, source_target_pairs={{0,16},{1,17},{2,18},{3,19},{4,20},{5,21},{6,22},{7,23},{8,24},{9,... | collective-permute-start | bytes 196616 | tf_op jit(solution)/shard_map/ppermute | solution.py:438
  106.9 0.1 pad_add_fusion.flags_ref
  107.0 0.8 collective-permute-done.12.other_ref
  107.8 0.0 collective-permute-done.13.refs_3_
  107.8 0.0 collective-permute-done.14.refs_7_
  107.8 5.4 %finish.1 = f32[12288,128]{1,0:T(8,128)} custom-call(s32[2]{0:T(128)S(1)} %pad_add_fusion.flags_ref, f32[128,128]{1,0:T(8,128)S(1)} %rotation.1.mine_ref, f32[128,128]{1,0:T(8,128)S(1)} %collective-permute-done.12.other_ref, f32[2816,128]{1,0:T(8,128)S(1)} %get-tuple-element.24.refs_0_, f32[2816,128]{1,0:T(8,128)S(1)} %get-tuple-element.25.own_ref.refs_1_, ...), custom_call_target="tpu_custom_call" | custom-call | tf_op jit(solution)/shard_map/finish/pallas_call | solution.py:413
  (9 shorter events, 0.1 us)
Async XLA Ops:
  0.0 26.5 %copy-start = (s32[16]{0:T(128)S(1)}, s32[16]{0:T(128)}, u32[]{:S(2)}) copy-start(s32[16]{0:T(128)} %param.3) | copy-start | bytes 196
  4.8 43.7 %collective-permute-start.5 = (f32[5632,128]{1,0:T(8,128)}, f32[5632,128]{1,0:T(8,128)S(1)}, u32[]{:S(2)}, u32[]{:S(2)}) collective-permute-start(f32[5632,128]{1,0:T(8,128)} %get-tuple-element.21.x_ref), channel_id=1, source_target_pairs={{0,1},{1,2},{2,3},{3,4},{4,5},{5,6},{6,7},{7,8},{8,9},{9,10},{10,1... | collective-permute-start | bytes 8650760 | tf_op jit(solution)/shard_map/ppermute | solution.py:438
  10.6 1.3 %collective-permute-start = (f32[128,128]{1,0:T(8,128)S(1)}, f32[128,128]{1,0:T(8,128)S(1)}, u32[]{:S(2)}, u32[]{:S(2)}) collective-permute-start(f32[128,128]{1,0:T(8,128)S(1)} %get-tuple-element.16), channel_id=1, source_target_pairs={{0,16},{1,17},{2,18},{3,19},{4,20},{5,21},{6,22},{7,23},{8,24},{9,... | collective-permute-start | bytes 196616 | tf_op jit(solution)/shard_map/ppermute | solution.py:438
  11.9 4.0 %collective-permute-start.1 = (f32[128,128]{1,0:T(8,128)S(1)}, f32[128,128]{1,0:T(8,128)S(1)}, u32[]{:S(2)}, u32[]{:S(2)}) collective-permute-start(f32[128,128]{1,0:T(8,128)S(1)} %add.33), channel_id=1, source_target_pairs={{0,32},{1,33},{2,34},{3,35},{4,36},{5,37},{6,38},{7,39},{8,40},{9,... | collective-permute-start | bytes 196616 | tf_op jit(solution)/shard_map/ppermute | solution.py:438
  15.9 5.0 %collective-permute-start.2 = (f32[128,128]{1,0:T(8,128)S(1)}, f32[128,128]{1,0:T(8,128)S(1)}, u32[]{:S(2)}, u32[]{:S(2)}) collective-permute-start(f32[128,128]{1,0:T(8,128)S(1)} %add.34), channel_id=1, source_target_pairs={{0,64},{1,65},{2,66},{3,67},{4,68},{5,69},{6,70},{7,71},{8,72},{9,... | collective-permute-start | bytes 196616 | tf_op jit(solution)/shard_map/ppermute | solution.py:438
  20.9 7.9 %collective-permute-start.3 = (f32[128,128]{1,0:T(8,128)S(1)}, f32[128,128]{1,0:T(8,128)S(1)}, u32[]{:S(2)}, u32[]{:S(2)}) collective-permute-start(f32[128,128]{1,0:T(8,128)S(1)} %add.35), channel_id=1, source_target_pairs={{0,224},{1,225},{2,226},{3,227},{4,228},{5,229},{6,230},{7,231},{8... | collective-permute-start | bytes 196616 | tf_op jit(solution)/shard_map/ppermute | solution.py:438
  41.2 21.4 %collective-permute-start.6 = (f32[3328,128]{1,0:T(8,128)S(1)}, f32[3328,128]{1,0:T(8,128)S(1)}, u32[]{:S(2)}, u32[]{:S(2)}) collective-permute-start(f32[3328,128]{1,0:T(8,128)S(1)} %get-tuple-element.18.refs_4_), channel_id=1, source_target_pairs={{0,1},{1,2},{2,3},{3,4},{4,5},{5,6},{6,7},{7,8},{8,9},{9,10},{10,1... | collective-permute-start | bytes 5111816 | tf_op jit(solution)/shard_map/ppermute | solution.py:438
  41.3 4.0 %collective-permute-start.4 = (f32[64,128]{1,0:T(8,128)S(1)}, f32[64,128]{1,0:T(8,128)S(1)}, u32[]{:S(2)}, u32[]{:S(2)}) collective-permute-start(f32[64,128]{1,0:T(8,128)S(1)} %get-tuple-element.19), channel_id=1, source_target_pairs={{0,31},{1,16},{2,17},{3,18},{4,19},{5,20},{6,21},{7,22},{8,23},{9,... | collective-permute-start | bytes 98312 | tf_op jit(solution)/shard_map/ppermute | solution.py:438
  62.6 45.2 %collective-permute-start.14 = (f32[3328,128]{1,0:T(8,128)S(1)}, f32[3328,128]{1,0:T(8,128)S(1)}, u32[]{:S(2)}, u32[]{:S(2)}) collective-permute-start(f32[3328,128]{1,0:T(8,128)S(1)} %get-tuple-element.26.own_ref.refs_5_), channel_id=1, source_target_pairs={{0,15},{1,0},{2,1},{3,2},{4,3},{5,4},{6,5},{7,6},{8,7},{9,8},{10,9... | collective-permute-start | bytes 5111816 | tf_op jit(solution)/shard_map/ppermute | solution.py:438
  62.6 45.2 %collective-permute-start.13 = (f32[2816,128]{1,0:T(8,128)S(1)}, f32[2816,128]{1,0:T(8,128)S(1)}, u32[]{:S(2)}, u32[]{:S(2)}) collective-permute-start(f32[2816,128]{1,0:T(8,128)S(1)} %get-tuple-element.25.own_ref.refs_1_), channel_id=1, source_target_pairs={{0,15},{1,0},{2,1},{3,2},{4,3},{5,4},{6,5},{7,6},{8,7},{9,8},{10,9... | collective-permute-start | bytes 4325384 | tf_op jit(solution)/shard_map/ppermute | solution.py:438
  63.9 7.3 %collective-permute-start.7 = (f32[128,128]{1,0:T(8,128)S(1)}, f32[128,128]{1,0:T(8,128)S(1)}, u32[]{:S(2)}, u32[]{:S(2)}) collective-permute-start(f32[128,128]{1,0:T(8,128)S(1)} %pair_gram.3), channel_id=1, source_target_pairs={{0,16},{1,17},{2,18},{3,19},{4,20},{5,21},{6,22},{7,23},{8,24},{9,... | collective-permute-start | bytes 196616 | tf_op jit(solution)/shard_map/ppermute | solution.py:438
  71.2 4.5 %collective-permute-start.8 = (f32[128,128]{1,0:T(8,128)S(1)}, f32[128,128]{1,0:T(8,128)S(1)}, u32[]{:S(2)}, u32[]{:S(2)}) collective-permute-start(f32[128,128]{1,0:T(8,128)S(1)} %collective-permute-done.7), channel_id=1, source_target_pairs={{0,1},{1,2},{2,3},{3,4},{4,5},{5,6},{6,7},{7,8},{8,9},{9,10},{10,1... | collective-permute-start | bytes 196616 | tf_op jit(solution)/shard_map/ppermute | solution.py:438
  75.7 3.5 %collective-permute-start.9 = (f32[128,128]{1,0:T(8,128)S(1)}, f32[128,128]{1,0:T(8,128)S(1)}, u32[]{:S(2)}, u32[]{:S(2)}) collective-permute-start(f32[128,128]{1,0:T(8,128)S(1)} %add.37), channel_id=1, source_target_pairs={{0,32},{1,33},{2,34},{3,35},{4,36},{5,37},{6,38},{7,39},{8,40},{9,... | collective-permute-start | bytes 196616 | tf_op jit(solution)/shard_map/ppermute | solution.py:438
  79.2 4.8 %collective-permute-start.10 = (f32[128,128]{1,0:T(8,128)S(1)}, f32[128,128]{1,0:T(8,128)S(1)}, u32[]{:S(2)}, u32[]{:S(2)}) collective-permute-start(f32[128,128]{1,0:T(8,128)S(1)} %add.38), channel_id=1, source_target_pairs={{0,64},{1,65},{2,66},{3,67},{4,68},{5,69},{6,70},{7,71},{8,72},{9,... | collective-permute-start | bytes 196616 | tf_op jit(solution)/shard_map/ppermute | solution.py:438
  84.0 4.6 %collective-permute-start.11 = (f32[128,128]{1,0:T(8,128)S(1)}, f32[128,128]{1,0:T(8,128)S(1)}, u32[]{:S(2)}, u32[]{:S(2)}) collective-permute-start(f32[128,128]{1,0:T(8,128)S(1)} %add.39), channel_id=1, source_target_pairs={{0,224},{1,225},{2,226},{3,227},{4,228},{5,229},{6,230},{7,231},{8... | collective-permute-start | bytes 196616 | tf_op jit(solution)/shard_map/ppermute | solution.py:438
  99.2 8.6 %collective-permute-start.12 = (f32[128,128]{1,0:T(8,128)S(1)}, f32[128,128]{1,0:T(8,128)S(1)}, u32[]{:S(2)}, u32[]{:S(2)}) collective-permute-start(f32[128,128]{1,0:T(8,128)S(1)} %rotation.1.mine_ref), channel_id=1, source_target_pairs={{0,16},{1,17},{2,18},{3,19},{4,20},{5,21},{6,22},{7,23},{8,24},{9,... | collective-permute-start | bytes 196616 | tf_op jit(solution)/shard_map/ppermute | solution.py:438
